TPU v7x, 512 devices: a whole 4x8x8 slice. The times are simulated.
512 devices in a mesh: seq: 64 (over y, x, core), chan: 8 (over z).
Axes of the slice: x: 4, y: 8, z: 8, core: 2. Of those that a mesh axis runs over, the one named last changes fastest.
Arguments:
- hidden_in: bfloat16 [8192, 8192], P('seq', 'chan'), as said below
- query_mr: bfloat16 [8192, 8192], P('seq', 'chan'), may hold values from -6 to 6
- key_mr: bfloat16 [8192, 8192], P('seq', 'chan'), may hold values from -6 to 6
- value_mr: bfloat16 [8192, 8192], P('seq', 'chan'), may hold values from -6 to 6
- query_li: bfloat16 [8192, 8192], P('seq', 'chan'), may hold values from -6 to 6
- key_li: bfloat16 [8192, 8192], P('seq', 'chan'), may hold values from -6 to 6
- mr_filter: bfloat16 [128, 512], P(None, 'chan'), may hold values from -0.5 to 0.5
- li_rate: float32 [16, 8192], P(None, 'chan'), as said below
- li_residue: float32 [16, 8192], P(None, 'chan'), may hold values from -4 to 4
- norm_gain: float32 [8192], P('chan'), may hold values from 0.25 to 1.75
Outputs:
- normed_out: bfloat16 [8192, 8192], P('seq', 'chan')
Inputs may be any that keep to these rules, and one draw needn't show every extreme that they name: `hidden_in`: real values of moderate size. `li_rate`: decay rates per position, all positive, from 1 / 81920 to 1 / 30.
All inputs are finite; a program needn't handle non-finite values.
Results may differ from a plain program's by a relative error of at most 0.0055.
Values may be sent and summed in bfloat16 or wider, within the bound.
No kernel may reach another device: no remote copies, remote signals or barrier semaphores. Data moves between devices by JAX's collectives and lax.ppermute only.
A program may use at most 64 MiB of HBM per device.

v0:
```python
import jax
import jax.numpy as jnp
from jax import lax
from jax.sharding import PartitionSpec as P


def passed_along(block, axis, distance):
    devices = range(lax.axis_size(axis))
    route = [(i - distance, i) for i in devices if i - distance in devices]
    return lax.ppermute(block, axis, route)


def band_matrix(filter_taps, filter_len):
    group_count = filter_taps.shape[1]
    padded = jnp.concatenate(
        [
            jnp.zeros((1, group_count), filter_taps.dtype),
            jnp.flip(filter_taps, 0),
            jnp.zeros((filter_len, group_count), filter_taps.dtype),
        ],
        0,
    )
    repeated = jnp.tile(padded, (filter_len, 1))[: filter_len * 2 * filter_len]
    return repeated.reshape(filter_len, 2 * filter_len, group_count)


def band_apply(toeplitz, earlier, latter, group_count):
    rows, channels = earlier.shape
    filter_len = toeplitz.shape[0]
    blocks = rows // filter_len
    earlier_rows = earlier.reshape(blocks, filter_len, group_count, channels // group_count)
    latter_rows = latter.reshape(blocks, filter_len, group_count, channels // group_count)
    windows = jnp.concatenate([earlier_rows, latter_rows], 1)
    result = jnp.einsum("tsg,bsgk->btgk", toeplitz, windows, preferred_element_type=jnp.float32)
    return result.reshape(rows, channels)


def per_device(
    hidden_in,
    query_mr,
    key_mr,
    value_mr,
    query_li,
    key_li,
    mr_filter,
    li_rate,
    li_residue,
    norm_gain,
):
    tokens, channels = key_mr.shape
    filter_len = mr_filter.shape[0]
    group_count = mr_filter.shape[1]
    highest = lax.Precision.HIGHEST
    product = (key_mr.astype(jnp.float32) * value_mr.astype(jnp.float32)).astype(jnp.bfloat16)
    toeplitz = band_matrix(mr_filter, filter_len)
    prior_rows = passed_along(product[tokens - filter_len + 1 :], "seq", 1)
    first_earlier = jnp.concatenate([jnp.zeros((1, channels), jnp.bfloat16), prior_rows], 0)
    earlier_all = jnp.concatenate([first_earlier, product[: tokens - filter_len]], 0)
    conv_mr = band_apply(toeplitz, earlier_all, product, group_count)
    out_mr = (query_mr.astype(jnp.float32) * conv_mr).astype(jnp.bfloat16)
    source = key_li.astype(jnp.float32) * out_mr.astype(jnp.float32)
    block_len = 16
    block_count = tokens // block_len
    scaled = li_residue * jnp.sqrt(-jnp.expm1(-2.0 * li_rate))
    lag_steps = jnp.arange(block_len).astype(jnp.float32)
    mode_taps = jnp.sum(scaled[None] * jnp.exp(-lag_steps[:, None, None] * li_rate[None]), 1)
    lag_index = jnp.arange(block_len)
    lag_grid = lag_index[:, None] - lag_index[None, :]
    selector = (lag_grid[:, :, None] == lag_index[None, None, :]).astype(jnp.float32)
    intra_block = jnp.einsum("tsd,dc->tsc", selector, mode_taps, precision=highest)
    decay_out = jnp.exp(-(block_len - 1 - lag_steps)[:, None, None] * li_rate[None])
    decay_in = scaled[None] * jnp.exp(-(lag_steps + 1.0)[:, None, None] * li_rate[None])
    blocks_in = source.reshape(block_count, block_len, channels)
    local_part = jnp.einsum("tsc,bsc->btc", intra_block, blocks_in, precision=highest)
    block_ends = jnp.einsum("snc,bsc->bnc", decay_out, blocks_in, precision=highest)
    block_decay = jnp.exp(-block_len * li_rate)

    def combine_blocks(earlier, latter):
        return (earlier[0] * latter[0], latter[0] * earlier[1] + latter[1])

    _, inclusive = lax.associative_scan(
        combine_blocks, (jnp.broadcast_to(block_decay[None], block_ends.shape), block_ends), axis=0
    )
    position = lax.axis_index("seq")
    shard_rows = lax.all_gather(inclusive[-1:], "seq", axis=0, tiled=True)
    owners = jnp.arange(shard_rows.shape[0], dtype=jnp.int32)
    distance = jnp.maximum(position - 1 - owners, 0).astype(jnp.float32)
    weight = jnp.where(
        (owners < position)[:, None, None],
        jnp.exp(-(tokens * distance)[:, None, None] * li_rate[None]),
        0.0,
    )
    incoming = jnp.sum(weight * shard_rows, 0)
    offsets = jnp.arange(block_count).astype(jnp.float32) * block_len
    start_states = (
        jnp.concatenate([jnp.zeros_like(inclusive[:1]), inclusive[:-1]], 0)
        + jnp.exp(-offsets[:, None, None] * li_rate[None]) * incoming[None]
    )
    from_states = jnp.einsum("tnc,bnc->btc", decay_in, start_states, precision=highest)
    conv_li = (local_part + from_states).reshape(tokens, channels)
    combined = (
        hidden_in.astype(jnp.float32)
        + out_mr.astype(jnp.float32)
        + query_li.astype(jnp.float32) * conv_li
    )
    local_squares = jnp.sum(combined * combined, axis=1)
    square_sum = lax.psum(local_squares, "chan")
    inverse_rms = lax.rsqrt(square_sum / (channels * lax.axis_size("chan")) + 1e-06)
    return (combined * inverse_rms[:, None] * norm_gain[None, :]).astype(jnp.bfloat16)


def solution(mesh):
    in_specs = (
        P("seq", "chan"),
        P("seq", "chan"),
        P("seq", "chan"),
        P("seq", "chan"),
        P("seq", "chan"),
        P("seq", "chan"),
        P(None, "chan"),
        P(None, "chan"),
        P(None, "chan"),
        P("chan"),
    )
    out_specs = P("seq", "chan")
    return jax.shard_map(
        per_device, mesh=mesh, in_specs=in_specs, out_specs=out_specs, check_vma=False
    )
```

profile of v0, /device:TPU:1, one launch (start us, length us, event | category | flops | bytes accessed | tf_op | source)
XLA Modules:
  0.0 192.0 jit_solution(13816346787504282258)
XLA Ops:
  6.5 0.0 all-gather.2.cloned.1.call-start
  6.5 1.1 multiply_convert_fusion.2
  7.6 0.1 slice.90
  7.7 4.5 %collective-permute-start = (bf16[127,1024]{1,0:T(8,128)(2,1)S(1)}, bf16[127,1024]{1,0:T(8,128)(2,1)S(1)}, u32[]{:S(2)}, u32[]{:S(2)}) collective-permute-start(bf16[127,1024]{1,0:T(8,128)(2,1)S(1)} %slice.90), channel_id=1, source_target_pairs={{0,8},{8,16},{16,24},{24,32},{32,40},{40,48},{48,56},{56,64},{64,7... | collective-permute-start | bytes 780296 | tf_op jit(solution)/shard_map/ppermute | solution.py:10
  12.2 0.8 rev.4
  13.0 0.1 pad.34.clone
  13.1 0.1 maximum_maximum_fusion
  13.2 0.2 copy.99
  13.4 3.2 %tile.4 = bf16[128,257,64]{1,0,2:T(8,128)(2,1)} broadcast(bf16[257,64]{0,1:T(8,128)(2,1)S(1)} %maximum_maximum_fusion), dimensions={1,2} | broadcast | bytes 4243584 | tf_op jit(solution)/shard_map/tile | solution.py:23
  16.6 10.8 %tile.10 = bf16[32896,64]{0,1:T(8,128)(2,1)} reshape(bf16[128,257,64]{1,0,2:T(8,128)(2,1)} %tile.4) | data formatting | bytes 8421376 | tf_op jit(solution)/shard_map/tile | solution.py:23
  27.4 0.0 slice-start
  27.4 2.2 %slice-done = bf16[32768,64]{0,1:T(8,128)(2,1)S(1)} async-done(((bf16[32896,64]{0,1:T(8,128)(2,1)}), bf16[32768,64]{0,1:T(8,128)(2,1)S(1)}, s32[]{:S(2)}) %slice-start) | async-done | bytes 4194328 | tf_op jit(solution)/shard_map/slice | solution.py:23
  29.6 0.0 copy-start
  29.6 0.0 copy-start.6
  29.6 3.0 %copy.113 = bf16[8,8,128,256]{3,2,1,0:T(8,128)(2,1)} copy(bf16[8,8,128,256]{3,1,2,0:T(8,128)(2,1)S(1)} %bitcast.43) | data formatting | bytes 8388608
  32.7 0.0 copy-done
  32.7 0.0 copy-start.4
  32.7 0.0 copy-start.5
  32.7 0.2 copy.102
  32.9 0.0 copy-done.6
  32.9 0.1 fusion.26
  32.9 0.0 collective-permute-done
  32.9 0.2 copy.112
  33.1 0.1 concatenate.18.clone
  33.3 3.4 %fusion.15 = f32[64,16,128]{2,1,0:T(8,128)S(1)} fusion(bf16[128,256,64]{1,0,2:T(8,128)(2,1)} %bitcast.44, bf16[1,128,64,16]{1,3,2,0:T(8,128)(2,1)S(1)} %bitcast.51, bf16[1,128,64,16]{1,3,2,0:T(8,128)(2,1)S(1)} %bitcast.50), kind=kOutput, calls=%fused_computation.19 | convolution fusion | flops 68157440 | bytes 5242880 | tf_op jit(solution)/shard_map/tsg,bsgk->btgk/dot_general | solution.py:34
  36.7 0.2 copy.100
  36.9 0.0 copy-done.4
  36.9 0.0 copy-done.5
  36.9 0.1 convert_multiply_fusion
  37.0 2.6 %copy.104 = f32[8,16,1024]{1,0,2:T(8,128)} copy(f32[8,16,1024]{2,1,0:T(8,128)S(1)} %bitcast.48) | data formatting | bytes 1048576 | tf_op jit(solution)/shard_map/reshape | solution.py:73
  39.6 11.1 %fusion.4 = f32[1024,8,16]{2,1,0:T(8,128)} fusion(f32[8,16,1024]{1,0,2:T(8,128)} %copy.104, f32[16]{0:T(128)S(1)} %subtract_negate_fusion, f32[16,1024]{0,1:T(8,128)S(1)} %copy.102), kind=kOutput, calls=%fused_computation.4 | convolution fusion | flops 25427968 | bytes 1114176 | tf_op jit(solution)/shard_map/snc,bsc->bnc/dot_general | solution.py:75
  50.7 2.8 %copy.107 = f32[1024,8,16]{0,2,1:T(8,128)S(1)} copy(f32[1024,8,16]{2,1,0:T(8,128)} %fusion.4) | data formatting | bytes 1048576 | tf_op jit(solution)/shard_map/snc,bsc->bnc/dot_general | solution.py:75
  53.8 0.0 copy-start.1
  53.8 0.1 pad.65
  53.9 0.6 slice.129
  54.5 0.0 all-gather.2.cloned.1.call-update
  54.5 0.0 copy-done.1
  54.6 0.2 copy.101
  54.8 3.5 %multiply_reduce_fusion = f32[16,1024]{0,1:T(8,128)S(1)} fusion(f32[16,1024]{0,1:T(8,128)S(1)} %copy.102, f32[16]{0:T(128)S(1)} %convert_negate_fusion, f32[16,1024]{0,1:T(8,128)S(1)} %copy.101), kind=kLoop, calls=%fused_computation.7 | loop fusion | flops 770048 | bytes 196672 | tf_op jit(solution)/shard_map/reduce_sum | solution.py:66
  58.3 0.6 fusion.18
  58.9 6.2 %copy.105 = f32[16,16,1024]{1,0,2:T(8,128)} copy(f32[16,16,1024]{2,1,0:T(8,128)S(1)} %fusion.18) | data formatting | bytes 2097152 | tf_op jit(solution)/shard_map/tsd,dc->tsc/dot_general | solution.py:70
  65.1 0.2 pad.26
  65.4 1.0 fusion.20
  66.4 0.1 pad.25
  66.4 0.1 slice_add_fusion
  66.5 17.5 %fusion.29 = f32[1024,8,16]{2,1,0:T(8,128)} fusion(f32[8,16,1024]{1,0,2:T(8,128)} %copy.104, f32[16,16,1024]{1,0,2:T(8,128)} %copy.105), kind=kOutput, calls=%fused_computation.62 | convolution fusion | flops 25165824 | bytes 2097152 | tf_op jit(solution)/shard_map/tsc,bsc->btc/dot_general | solution.py:74
  84.0 59.4 %all-gather.2.cloned.1.call-done = f32[64,16,1024]{2,1,0:T(8,128)} async-done(((f32[1,16,1024]{2,1,0:T(8,128)}), f32[64,16,1024]{2,1,0:T(8,128)}) %all-gather.2.cloned.1.call-update) | async-done | bytes 4194320 | tf_op jit(solution)/shard_map/all_gather | solution.py:85
  143.3 3.1 %multiply_reduce_fusion.1 = f32[16,1024]{1,0:T(8,128)S(1)} fusion(f32[64,16,1024]{2,1,0:T(8,128)} %all-gather.2.cloned.1.call-done, f32[16,1024]{1,0:T(8,128)S(1)} %copy-done, f32[64]{0:T(128)S(1)} %multiply_negate_fusion, pred[64]{0:T(512)(128)(4,1)S(1)} %iota_compare_fusion.2), kind=kLoop, calls=%fused_computation.10 | loop fusion | flops 4177920 | bytes 4325696 | tf_op jit(solution)/shard_map/reduce_sum | solution.py:93
  146.5 0.2 multiply_add_fusion
  146.6 2.6 %copy.108 = f32[8,16,1024]{1,0,2:T(8,128)} copy(f32[8,16,1024]{2,1,0:T(8,128)S(1)} %multiply_add_fusion) | data formatting | bytes 1048576 | tf_op jit(solution)/shard_map/add | solution.py:96
  149.2 17.5 %add_bitcast_fusion = f32[8,16,1024]{1,0,2:T(8,128)} fusion(f32[1024,8,16]{2,1,0:T(8,128)} %fusion.29, f32[8,16,1024]{1,0,2:T(8,128)} %copy.108, f32[16]{0:T(128)S(1)} %add_negate_fusion, f32[16,1024]{0,1:T(8,128)S(1)} %copy.102, f32[16,1024]{0,1:T(8,128)S(1)} %copy.101), kind=kOutput, calls=%fused_computation.8 | convolution fusion | flops 25821184 | bytes 1704000 | tf_op jit(solution)/shard_map/tnc,bnc->btc/dot_general | solution.py:99
  166.7 0.0 copy-start.2
  166.7 0.0 copy-start.3
  166.7 0.0 copy-start.7
  166.7 2.9 %copy.109 = f32[8,16,1024]{2,1,0:T(8,128)S(1)} copy(f32[8,16,1024]{1,0,2:T(8,128)} %add_bitcast_fusion) | data formatting | bytes 1048576 | tf_op jit(solution)/shard_map/add | solution.py:100
  169.6 0.0 copy-done.2
  169.6 0.0 copy-done.3
  169.6 0.2 multiply_reduce_fusion.2
  169.8 14.4 %psum.7 = f32[128]{0:T(128)S(1)} all-reduce(f32[128]{0:T(128)S(1)} %multiply_reduce_fusion.2), channel_id=1, replica_groups=mesh['seq'=64,'chan'=8] {'chan'}, use_global_device_ids=true, to_apply=%region_3.4 | all-reduce | flops 128 | bytes 1024 | tf_op jit(solution)/shard_map/psum | solution.py:107
  184.3 0.0 copy-done.7
  184.3 0.9 multiply_convert_fusion
  (21 shorter events, 0.3 us)
Async XLA Ops:
  6.5 136.8 %all-gather.2.cloned.1.call-start = ((), (), s32[]{:S(2)}) async-start(), calls=%async_computation | async-start | bytes 4259840 | tf_op jit(solution)/shard_map/all_gather | solution.py:85
  7.7 25.2 %collective-permute-start = (bf16[127,1024]{1,0:T(8,128)(2,1)S(1)}, bf16[127,1024]{1,0:T(8,128)(2,1)S(1)}, u32[]{:S(2)}, u32[]{:S(2)}) collective-permute-start(bf16[127,1024]{1,0:T(8,128)(2,1)S(1)} %slice.90), channel_id=1, source_target_pairs={{0,8},{8,16},{16,24},{24,32},{32,40},{40,48},{48,56},{56,64},{64,7... | collective-permute-start | bytes 780296 | tf_op jit(solution)/shard_map/ppermute | solution.py:10
  27.4 2.2 %slice-start = ((bf16[32896,64]{0,1:T(8,128)(2,1)}), bf16[32768,64]{0,1:T(8,128)(2,1)S(1)}, s32[]{:S(2)}) async-start(bf16[32896,64]{0,1:T(8,128)(2,1)} %tile.10), calls=%async_computation.1 | async-start | bytes 8388608 | tf_op jit(solution)/shard_map/slice | solution.py:23
  29.6 3.0 %copy-start = (f32[16,1024]{1,0:T(8,128)S(1)}, f32[16,1024]{1,0:T(8,128)}, u32[]{:S(2)}) copy-start(f32[16,1024]{1,0:T(8,128)} %param.17) | copy-start | bytes 196612
  29.6 3.2 %copy-start.6 = (f32[16,1024]{1,0:T(8,128)S(1)}, f32[16,1024]{1,0:T(8,128)}, u32[]{:S(2)}) copy-start(f32[16,1024]{1,0:T(8,128)} %param.18) | copy-start | bytes 196612
  32.7 4.2 %copy-start.4 = (bf16[128,1024]{1,0:T(8,128)(2,1)S(1)}, bf16[128,1024]{1,0:T(8,128)(2,1)}, u32[]{:S(2)}) copy-start(bf16[128,1024]{1,0:T(8,128)(2,1)} %param.15) | copy-start | bytes 786436
  32.7 4.2 %copy-start.5 = (bf16[128,1024]{1,0:T(8,128)(2,1)S(1)}, bf16[128,1024]{1,0:T(8,128)(2,1)}, u32[]{:S(2)}) copy-start(bf16[128,1024]{1,0:T(8,128)(2,1)} %param.11) | copy-start | bytes 786436
  53.8 0.8 copy-start.1
  166.7 2.9 %copy-start.2 = (bf16[128,1024]{1,0:T(8,128)(2,1)S(1)}, bf16[128,1024]{1,0:T(8,128)(2,1)}, u32[]{:S(2)}) copy-start(bf16[128,1024]{1,0:T(8,128)(2,1)} %param.14) | copy-start | bytes 786436
  166.7 2.9 %copy-start.3 = (bf16[128,1024]{1,0:T(8,128)(2,1)S(1)}, bf16[128,1024]{1,0:T(8,128)(2,1)}, u32[]{:S(2)}) copy-start(bf16[128,1024]{1,0:T(8,128)(2,1)} %param.10) | copy-start | bytes 786436
  166.7 17.5 %copy-start.7 = (f32[1024]{0:T(1024)S(1)}, f32[1024]{0:T(1024)}, u32[]{:S(2)}) copy-start(f32[1024]{0:T(1024)} %param.19) | copy-start | bytes 12292
Sparse Core Ops, SparseCore 0:
  54.7 88.6 all-gather.1
where the time goes:
time: 194 us; the launch traced here: 192 us
  waiting for transfers between devices  59.4 us (31%)
  matrix products  50 us (26%)
  local copies, waits for them, and re-layouts  39.5 us (20%)
  blocking collectives  14.4 us (7%)
  between operations  13.7 us (7%)
  other arithmetic  10.4 us (5%)
  starting transfers between devices  4.51 us (2%)
    all_gather x1, waiting for transfers between devices, per_device(): shard_rows = lax.all_gather(inclusive[-1:], 'seq', axis=0, tiled=True)  59.4 us
    dot_general x1, matrix products, per_device(): jnp.einsum('tnc,bnc->btc', decay_in, start_states, precision=highest)  17.5 us
    dot_general x1, matrix products, per_device(): jnp.einsum('tsc,bsc->btc', intra_block, blocks_in, precision=highest)  17.5 us
    psum x1, blocking collectives, per_device(): square_sum = lax.psum(local_squares, 'chan')  14.4 us
    another operation x2, local copies, waits for them, and re-layouts, band_matrix(): repeated = jnp.tile(padded, (filter_len, 1))[:filter_len * 2 * filter_len]  14 us
    dot_general x1, matrix products, per_device(): jnp.einsum('snc,bsc->bnc', decay_out, blocks_in, precision=highest)  11.1 us
    dot_general x1, local copies, waits for them, and re-layouts, per_device(): jnp.einsum('tsd,dc->tsc', selector, mode_taps, precision=highest)  6.16 us
    ppermute x1, starting transfers between devices, passed_along(): return lax.ppermute(block, axis, route)  4.51 us
  transfers between devices with their start and end apart: 2, of which 1 were waited for; matrix products, arithmetic and copies ran while one was open for 25% of the time, Pallas kernels for 0%

commit v1 on v0

v1 whole, which is shorter than its diff:
```python
import jax
import jax.numpy as jnp
from jax import lax
from jax.experimental import pallas as pl
from jax.experimental.pallas import tpu as pltpu
from jax.sharding import Mesh, PartitionSpec as P

F32 = jnp.float32
BF16 = jnp.bfloat16
LANES = 128
SUBS = 8
STEP = 16
SEQ = ("y", "x", "core")
HIGHEST = lax.Precision.HIGHEST
VMEM_LIMIT = 48 * 1024 * 1024


def iota(shape, dim):
    return lax.broadcasted_iota(jnp.int32, shape, dim)


def strided(row):
    return pl.ds(row, SUBS, stride=STEP)


def tile_cols(tile):
    return pl.ds(tile * LANES, LANES)


def spread_row(values, n):
    return jnp.broadcast_to(values[n : n + 1], (SUBS, LANES))


def own_kernel(filter_ref, product_ref, table_ref, bands_ref, conv_ref, taps_ref):
    groups, taps = filter_ref.shape
    channels = product_ref.shape[1]
    width = channels // groups
    per_tile = LANES // width
    row, lane = iota((taps, taps), 0), iota((taps, taps), 1)
    flip = ((row + lane) % taps == 0).astype(BF16)
    flipped = jnp.dot(filter_ref[...], flip, preferred_element_type=F32)
    earlier = lane > row
    lane_group = iota((taps, LANES), 1) // width
    for tile in range(channels // LANES):
        cols = tile_cols(tile)
        latest = product_ref[:, cols]
        conv = jnp.zeros((taps, LANES), F32)
        for part in range(per_tile):
            group = tile * per_tile + part
            one = jnp.broadcast_to(flipped[group : group + 1], (taps, taps))
            circulant = pltpu.roll(one, 0, 1, stride=1, stride_axis=0)
            bands_ref[group] = jnp.where(earlier, circulant, 0.0).astype(BF16)
            band = jnp.where(earlier, 0.0, circulant).astype(BF16)
            result = jnp.dot(band, latest, preferred_element_type=F32)
            conv = jnp.where(lane_group == part, result, conv)
        conv_ref[:, cols] = conv
        decay = jnp.exp(table_ref[1, :, cols] / STEP)
        powers = table_ref[0, :, cols]
        for lag in range(STEP):
            taps_ref[lag : lag + 1, cols] = jnp.sum(powers, 0, keepdims=True)
            powers = powers * decay


def medium_kernel(
    halo_ref, bands_ref, conv_ref, query_ref, key_ref, table_ref,
    out_mr_ref, source_ref, starts_ref, spread_ref,
):
    tokens, channels = halo_ref.shape
    groups = bands_ref.shape[0]
    poles = table_ref.shape[1]
    width = channels // groups
    per_tile = LANES // width
    lane_group = iota((tokens, LANES), 1) // width
    block = iota((SUBS, LANES), 0)
    for tile in range(channels // LANES):
        cols = tile_cols(tile)
        before = halo_ref[:, cols]
        conv = jnp.zeros((tokens, LANES), F32)
        for part in range(per_tile):
            band = bands_ref[tile * per_tile + part]
            result = jnp.dot(band, before, preferred_element_type=F32)
            conv = jnp.where(lane_group == part, result, conv)
        conv = conv + conv_ref[:, cols]
        out_mr = (query_ref[:, cols].astype(F32) * conv).astype(BF16)
        out_mr_ref[:, cols] = out_mr
        source_ref[tile] = key_ref[:, cols].astype(F32) * out_mr.astype(F32)
        gain, fade = table_ref[0, :, cols], table_ref[1, :, cols]
        decay = jnp.exp(fade / STEP)
        jumps = [jnp.exp(fade * k) for k in (1, 2, 4)]
        rows = [source_ref[tile, strided(i), :] for i in range(STEP)]
        last = []
        for n in range(poles):
            one = spread_row(decay, n)
            ends = rows[0]
            for i in range(1, STEP):
                ends = ends * one + rows[i]
            for k, jump in zip((1, 2, 4), jumps):
                shifted = jnp.where(block >= k, pltpu.roll(ends, k, 0), 0.0)
                ends = ends + spread_row(jump, n) * shifted
            shifted = jnp.where(block >= 1, pltpu.roll(ends, 1, 0), 0.0)
            starts_ref[n, :, cols] = shifted * spread_row(gain, n)
            last.append(ends[SUBS - 1 :])
        state = jnp.concatenate(last, 0).astype(BF16)
        half = spread_ref.shape[2]
        for to in range(tile * LANES // half, spread_ref.shape[0], 2):
            spread_ref[to, :, pl.ds(tile * LANES % half, LANES)] = state


def own_half(tile, half):
    start = lax.axis_index("core") * half + tile * LANES
    return pl.ds(pl.multiple_of(start, LANES), LANES)


def scan_stack(stack_ref, cols, step):
    states = [jnp.zeros(step.shape, F32)]
    for j in range(stack_ref.shape[0]):
        states.append(states[-1] * step + stack_ref[j, :, cols].astype(F32))
    return states


def pick(states, position):
    chosen = states[0]
    for j in range(1, len(states)):
        chosen = jnp.where(position == j, states[j], chosen)
    return chosen


def row_kernel(tokens, stack_ref, table_ref, ahead_ref, spread_ref):
    half = stack_ref.shape[2]
    place = lax.axis_index("x")
    for tile in range(half // LANES):
        cols = tile_cols(tile)
        step = jnp.exp(table_ref[1, :, own_half(tile, half)] * (tokens // STEP))
        states = scan_stack(stack_ref, cols, step)
        for core in range(2):
            ahead_ref[core, :, cols] = pick(states[core:-1:2], place)
        state = states[-1].astype(BF16)
        for to in range(spread_ref.shape[0]):
            spread_ref[to, :, cols] = state


def join_kernel(tokens, stack_ref, ahead_ref, table_ref, incoming_ref):
    half = stack_ref.shape[2]
    in_row = lax.axis_size("x") * 2
    first = (lax.axis_index("x") * 2).astype(F32)
    for tile in range(half // LANES):
        cols = tile_cols(tile)
        fade = table_ref[1, :, own_half(tile, half)] * (tokens // STEP)
        states = scan_stack(stack_ref, cols, jnp.exp(fade * in_row))
        above = pick(states[:-1], lax.axis_index("y"))
        for core in range(2):
            reach = jnp.exp(fade * (first + core))
            incoming_ref[core, :, cols] = ahead_ref[core, :, cols] + reach * above


def long_kernel(
    incoming_ref, table_ref, taps_ref, source_ref, starts_ref,
    hidden_ref, out_mr_ref, query_ref, norm_ref,
    scaled_ref, squares_ref, conv_ref,
):
    tokens, channels = hidden_ref.shape
    poles = table_ref.shape[1]
    half = incoming_ref.shape[3]
    core = lax.axis_index("core")
    block = iota((SUBS, LANES), 0).astype(F32)
    squares = jnp.zeros((tokens, LANES), F32)
    for tile in range(channels // LANES):
        cols = tile_cols(tile)
        gain, fade = table_ref[0, :, cols], table_ref[1, :, cols]
        decay = jnp.exp(fade / STEP)
        place = tile * LANES
        incoming = incoming_ref[place // half, core, :, pl.ds(place % half, LANES)] * gain
        rows = [source_ref[tile, strided(i), :] for i in range(STEP)]
        sums = [jnp.zeros((SUBS, LANES), F32)] * STEP
        for lag in range(STEP):
            tap = jnp.broadcast_to(taps_ref[lag : lag + 1, cols], (SUBS, LANES))
            for i in range(lag, STEP):
                sums[i] = sums[i] + tap * rows[i - lag]
        for n in range(poles):
            one = spread_row(decay, n)
            entering = jnp.exp(block * spread_row(fade, n)) * spread_row(incoming, n)
            mode = starts_ref[n, :, cols] + entering
            for i in range(STEP):
                mode = mode * one
                sums[i] = sums[i] + mode
        for i in range(STEP):
            conv_ref[strided(i), :] = sums[i]
        combined = (
            hidden_ref[:, cols].astype(F32)
            + out_mr_ref[:, cols].astype(F32)
            + query_ref[:, cols].astype(F32) * conv_ref[...]
        )
        scaled_ref[:, cols] = combined * norm_ref[:, cols]
        squares = squares + combined * combined
    total = jnp.sum(squares.T, 0, keepdims=True)
    squares_ref[...] = jnp.broadcast_to(total, squares_ref.shape)


def call(kernel, outs, scratch=(), cost=None):
    return pl.pallas_call(
        kernel,
        out_shape=[jax.ShapeDtypeStruct(shape, dtype) for shape, dtype in outs],
        scratch_shapes=[pltpu.VMEM(shape, dtype) for shape, dtype in scratch],
        compiler_params=pltpu.CompilerParams(vmem_limit_bytes=VMEM_LIMIT),
        cost_estimate=cost,
    )


def per_device(
    hidden_in,
    query_mr,
    key_mr,
    value_mr,
    query_li,
    key_li,
    mr_filter,
    li_rate,
    li_residue,
    norm_gain,
):
    tokens, channels = key_mr.shape
    filter_len, groups = mr_filter.shape
    poles = li_rate.shape[0]
    tiles = channels // LANES
    half = channels // 2
    ys = lax.axis_size("y")
    in_row = lax.axis_size("x") * lax.axis_size("core")
    product = (key_mr.astype(F32) * value_mr.astype(F32)).astype(BF16)
    halo = lax.ppermute(product, SEQ, [(i, i + 1) for i in range(ys * in_row - 1)])
    gain = li_residue * jnp.sqrt(-jnp.expm1(-2.0 * li_rate))
    table = jnp.stack([gain, li_rate * -float(STEP)])
    cost = pl.CostEstimate(
        flops=2 * groups * filter_len * filter_len * LANES, bytes_accessed=2**22, transcendentals=0
    )
    bands, own, taps = call(
        own_kernel,
        [
            ((groups, filter_len, filter_len), BF16),
            ((tokens, channels), F32),
            ((STEP, channels), F32),
        ],
        cost=cost,
    )(mr_filter.T, product, table)
    out_mr, source, starts, states = call(
        medium_kernel,
        [
            ((tokens, channels), BF16),
            ((tiles, tokens, LANES), F32),
            ((poles, SUBS, channels), F32),
            ((in_row, poles, half), BF16),
        ],
    )(halo, bands, own, query_mr, key_li, table)
    states = lax.all_to_all(states, ("x", "core"), 0, 0, tiled=True)
    ahead, rows = call(
        lambda *refs: row_kernel(tokens, *refs),
        [((2, poles, half), F32), ((ys, poles, half), BF16)],
    )(states, table)
    rows = lax.all_to_all(rows, "y", 0, 0, tiled=True)
    (incoming,) = call(lambda *refs: join_kernel(tokens, *refs), [((2, poles, half), F32)])(
        rows, ahead, table
    )
    incoming = lax.all_gather(incoming, "core")
    scaled, squares = call(
        long_kernel,
        [((tokens, channels), F32), ((SUBS, tokens), F32)],
        [((tokens, LANES), F32)],
    )(
        incoming, table, taps, source, starts,
        hidden_in, out_mr, query_li, norm_gain.reshape(1, channels),
    )
    chans = lax.axis_size("chan")
    squares = lax.all_to_all(squares.reshape(chans, 1, tokens), "chan", 0, 0, tiled=True)
    inverse_rms = lax.rsqrt(jnp.sum(squares, (0, 1)) / (channels * chans) + 1e-06)
    return (scaled * inverse_rms[:, None]).astype(BF16)


def solution(mesh):
    seq, chan = mesh.devices.shape
    xs = 4 if seq >= 64 else 2
    fine = Mesh(mesh.devices.reshape(seq // (2 * xs), xs, 2, chan), ("y", "x", "core", "chan"))
    both = P(SEQ, "chan")
    last = P(None, "chan")
    return jax.shard_map(
        per_device,
        mesh=fine,
        in_specs=(both,) * 6 + (last,) * 3 + (P("chan"),),
        out_specs=both,
        check_vma=False,
    )
```

time: 194 us -> 60.7 us (0.31)
  waiting for transfers between devices: 59.4 us -> 1.66 us
  matrix products: 50 us -> 0 us
  local copies, waits for them, and re-layouts: 39.5 us -> 0.73 us
  blocking collectives: 14.4 us -> 45.8 us
  between operations: 13.7 us -> 0.07 us
  other arithmetic: 10.4 us -> 2.93 us
  Pallas kernels: 0 us -> 4.73 us
    all_gather x1 -> x0, waiting for transfers between devices: 59.4 us -> none  [per_device(): shard_rows = lax.all_gather(inclusive[-1:], 'seq', axis=0, tiled=True)]
    dot_general x5 -> x0, matrix products: 50 us -> none  [the longest x1 17.5 us: per_device(): jnp.einsum('tnc,bnc->btc', decay_in, start_states, precision=highest)]
    all_to_all x0 -> x3, blocking collectives: none -> 41.8 us  [the longest x1 16.4 us: per_device(): lax.all_to_all(squares.reshape(chans, 1, tokens), 'chan', 0, 0, tiled=True)]
    psum x1 -> x0, blocking collectives: 14.4 us -> none  [per_device(): square_sum = lax.psum(local_squares, 'chan')]
    another operation x2 -> x0, local copies, waits for them, and re-layouts: 14 us -> none  [band_matrix(): repeated = jnp.tile(padded, (filter_len, 1))[:filter_len * 2 * filter_len]]
    dot_general x2 -> x0, local copies, waits for them, and re-layouts: 8.95 us -> none  [the longest x1 6.16 us: per_device(): jnp.einsum('tsd,dc->tsc', selector, mode_taps, precision=highest)]
    reduce_sum x3 -> x1, other arithmetic: 6.85 us -> 0.03 us  [per_device(): jnp.sum(squares, (0, 1)) / (channels * chans) + 1e-06]
    add x2 -> x0, local copies, waits for them, and re-layouts: 5.48 us -> none  [the longest x1 2.85 us: per_device(): conv_li = (local_part + from_states).reshape(tokens, channels)]
  transfers between devices with their start and end apart: 2 -> 1, of which waited for: 1 -> 1; matrix products, arithmetic and copies ran while one was open for 25% -> 2% of each run, Pallas kernels for 0% -> 2%
where the time goes in v1:
time: 60.7 us; the launch traced here: 60.4 us
  blocking collectives  45.8 us (75%)
  Pallas kernels  4.73 us (8%)
  starting transfers between devices  4.51 us (7%)
  other arithmetic  2.93 us (5%)
  waiting for transfers between devices  1.66 us (3%)
  local copies, waits for them, and re-layouts  0.73 us (1%)
    all_to_all x1, blocking collectives, per_device(): lax.all_to_all(squares.reshape(chans, 1, tokens), 'chan', 0, 0, tiled=True)  16.4 us
    all_to_all x1, blocking collectives, per_device(): rows = lax.all_to_all(rows, 'y', 0, 0, tiled=True)  15.7 us
    all_to_all x1, blocking collectives, per_device(): states = lax.all_to_all(states, ('x', 'core'), 0, 0, tiled=True)  9.72 us
    ppermute x1, starting transfers between devices, per_device(): lax.ppermute(product, SEQ, [(i, i + 1) for i in range(ys * in_row - 1)])  4.51 us
    all_gather x1, blocking collectives, per_device(): incoming = lax.all_gather(incoming, 'core')  3.92 us
    pallas_call x1, Pallas kernels, per_device(): call(medium_kernel, [((tokens, channels), BF16), ((tiles, tokens, LANES),...  1.84 us
    ppermute x1, waiting for transfers between devices, per_device(): lax.ppermute(product, SEQ, [(i, i + 1) for i in range(ys * in_row - 1)])  1.66 us
    pallas_call x1, Pallas kernels, per_device(): call(long_kernel, [((tokens, channels), F32), ((SUBS, tokens), F32)], [((...  1.43 us
  transfers between devices with their start and end apart: 1, of which 1 were waited for; matrix products, arithmetic and copies ran while one was open for 2% of the time, Pallas kernels for 2%

profile of v1, /device:TPU:1, one launch (start us, length us, event | category | flops | bytes accessed | tf_op | source)
XLA Modules:
  0.0 60.4 jit_solution(14881874808257410380)
XLA Ops:
  0.0 0.0 copy-start.1
  0.0 0.0 copy-start
  0.0 1.2 %multiply_convert_fusion.1.product_ref = bf16[128,1024]{1,0:T(8,128)(2,1)S(1)} fusion(bf16[128,1024]{1,0:T(8,128)(2,1)} %param.13, bf16[128,1024]{1,0:T(8,128)(2,1)} %param.12), kind=kLoop, calls=%fused_computation.1 | loop fusion | flops 524288 | bytes 786432 | tf_op jit(solution)/shard_map/convert_element_type | solution.py:228
  1.2 4.5 %collective-permute-start = (bf16[128,1024]{1,0:T(8,128)(2,1)S(1)}, bf16[128,1024]{1,0:T(8,128)(2,1)S(1)}, u32[]{:S(2)}, u32[]{:S(2)}) collective-permute-start(bf16[128,1024]{1,0:T(8,128)(2,1)S(1)} %multiply_convert_fusion.1.product_ref), channel_id=1, source_target_pairs={{0,8},{8,16},{16,24},{24,32},{32,40},{40,48},{48,56},{56,64},{64,7... | collective-permute-start | bytes 786440 | tf_op jit(solution)/shard_map/ppermute | solution.py:229
  5.7 0.9 %multiply_bitcast_fusion.1 = (f32[1,16,1024]{2,1,0:T(8,128)S(1)}, f32[1,16,1024]{2,1,0:T(8,128)S(1)}) fusion(f32[16,1024]{1,0:T(8,128)} %param.18, f32[16,1024]{1,0:T(8,128)} %param.17), kind=kLoop, calls=%fused_computation.4 | loop fusion | flops 65536 | bytes 262144 | tf_op jit(solution)/shard_map/stack | solution.py:231
  6.6 0.0 copy-start.5
  6.6 0.7 %copy-done.5 = bf16[128,64]{0,1:T(8,128)(2,1)S(1)} copy-done((bf16[128,64]{0,1:T(8,128)(2,1)S(1)}, bf16[128,64]{0,1:T(8,128)(2,1)}, u32[]{:S(2)}) %copy-start.5) | copy-done | bytes 16408
  7.3 1.3 %shard_map.100 = (bf16[64,128,128]{2,1,0:T(8,128)(2,1)S(1)}, f32[128,1024]{1,0:T(8,128)S(1)}, f32[16,1024]{1,0:T(8,128)S(1)}) custom-call(bf16[64,128]{1,0:T(8,128)(2,1)S(1)} %bitcast.13, bf16[128,1024]{1,0:T(8,128)(2,1)S(1)} %multiply_convert_fusion.1.product_ref, f32[2,16,1024]{2,1,0:T(8,128)S(1)} %pad_maximum_fusion.table_ref.refs_1_.refs_2_), custom_call_target="tpu_custom_call" | custom-call | flops 268435456 | bytes 4194304 | tf_op jit(solution)/shard_map/pallas_call | solution.py:235
  8.7 1.7 %collective-permute-done.halo_ref = bf16[128,1024]{1,0:T(8,128)(2,1)S(1)} collective-permute-done((bf16[128,1024]{1,0:T(8,128)(2,1)S(1)}, bf16[128,1024]{1,0:T(8,128)(2,1)S(1)}, u32[]{:S(2)}, u32[]{:S(2)}) %collective-permute-start) | collective-permute-done | bytes 262176 | tf_op jit(solution)/shard_map/ppermute | solution.py:229
  10.3 0.0 copy-done.1
  10.3 0.0 copy-done
  10.4 0.0 copy-start.2
  10.4 0.0 copy-start.3
  10.4 0.0 copy-start.4
  10.4 1.8 %shard_map.101 = (bf16[128,1024]{1,0:T(8,128)(2,1)S(1)}, f32[8,128,128]{2,1,0:T(8,128)S(1)}, f32[16,8,1024]{2,1,0:T(8,128)S(1)}, bf16[8,16,512]{2,1,0:T(8,128)(2,1)S(1)}) custom-call(bf16[128,1024]{1,0:T(8,128)(2,1)S(1)} %collective-permute-done.halo_ref, bf16[64,128,128]{2,1,0:T(8,128)(2,1)S(1)} %get-tuple-element.16.bands_ref, ...), custom_call_target="tpu_custom_call" | custom-call | tf_op jit(solution)/shard_map/pallas_call | solution.py:244
  12.2 9.7 %all_to_all.15.refs_0_ = bf16[8,16,512]{2,1,0:T(8,128)(2,1)S(1)} all-to-all(bf16[8,16,512]{2,1,0:T(8,128)(2,1)S(1)} %get-tuple-element.18), channel_id=1, replica_groups=mesh['y'=8,'x'=4,'core'=2,'chan'=8] {'x','core'}, dimensions={0} | all-to-all | bytes 262144 | tf_op jit(solution)/shard_map/all_to_all | solution.py:253
  21.9 0.1 shard_map.102
  22.0 15.7 %all_to_all.16.refs_0_ = bf16[8,16,512]{2,1,0:T(8,128)(2,1)S(1)} all-to-all(bf16[8,16,512]{2,1,0:T(8,128)(2,1)S(1)} %get-tuple-element.19), channel_id=1, replica_groups=mesh['y'=8,'x'=4,'core'=2,'chan'=8] {'y'}, dimensions={0} | all-to-all | bytes 262144 | tf_op jit(solution)/shard_map/all_to_all | solution.py:258
  37.7 0.1 shard_map.103
  37.8 3.9 %all-gather = f32[4,16,512]{2,1,0:T(8,128)S(1)} all-gather(f32[2,16,512]{2,1,0:T(8,128)S(1)} %shard_map.103), channel_id=2, replica_groups=mesh['y'=8,'x'=4,'core'=2,'chan'=8] {'core'}, dimensions={0}, use_global_device_ids=true | all-gather | bytes 196608 | tf_op jit(solution)/shard_map/all_gather | solution.py:262
  41.7 0.0 copy-done.2
  41.7 0.0 copy-done.3
  41.7 0.0 copy-done.4
  41.7 1.4 %shard_map.104 = (f32[128,1024]{1,0:T(8,128)S(1)}, f32[8,128]{1,0:T(8,128)S(1)}) custom-call(f32[2,2,16,512]{3,2,1,0:T(8,128)S(1)} %bitcast.10, f32[2,16,1024]{2,1,0:T(8,128)S(1)} %pad_maximum_fusion.table_ref.refs_1_.refs_2_, f32[16,1024]{1,0:T(8,128)S(1)} %get-tuple-element.21.taps_ref, f32[8,128,128]{2,1,0:T(8,128)S(1)} %get-tuple-element.22.source_ref, ...), custom_call_target="tpu_custom_call" | custom-call | tf_op jit(solution)/shard_map/pallas_call | solution.py:263
  43.2 16.4 %all_to_all.17 = f32[8,1,128]{2,1,0:T(1,128)S(1)} all-to-all(f32[8,1,128]{2,1,0:T(1,128)S(1)} %bitcast.12), channel_id=1, replica_groups=mesh['y'=8,'x'=4,'core'=2,'chan'=8] {'chan'}, dimensions={0} | all-to-all | bytes 8192 | tf_op jit(solution)/shard_map/all_to_all | solution.py:272
  59.6 0.8 %multiply_convert_fusion = bf16[128,1024]{1,0:T(8,128)(2,1)} fusion(f32[128,1024]{1,0:T(8,128)S(1)} %get-tuple-element.25, f32[128]{0:T(128)S(1)} %add_rsqrt_fusion), kind=kLoop, calls=%fused_computation | loop fusion | flops 262144 | bytes 786944 | tf_op jit(solution)/shard_map/convert_element_type | solution.py:274
  (3 shorter events, 0.0 us)
Async XLA Ops:
  0.0 10.3 %copy-start.1 = (bf16[128,1024]{1,0:T(8,128)(2,1)S(1)}, bf16[128,1024]{1,0:T(8,128)(2,1)}, u32[]{:S(2)}) copy-start(bf16[128,1024]{1,0:T(8,128)(2,1)} %key_ref.1) | copy-start | bytes 786436
  0.0 10.3 %copy-start = (bf16[128,1024]{1,0:T(8,128)(2,1)S(1)}, bf16[128,1024]{1,0:T(8,128)(2,1)}, u32[]{:S(2)}) copy-start(bf16[128,1024]{1,0:T(8,128)(2,1)} %query_ref.2) | copy-start | bytes 786436
  1.2 9.2 %collective-permute-start = (bf16[128,1024]{1,0:T(8,128)(2,1)S(1)}, bf16[128,1024]{1,0:T(8,128)(2,1)S(1)}, u32[]{:S(2)}, u32[]{:S(2)}) collective-permute-start(bf16[128,1024]{1,0:T(8,128)(2,1)S(1)} %multiply_convert_fusion.1.product_ref), channel_id=1, source_target_pairs={{0,8},{8,16},{16,24},{24,32},{32,40},{40,48},{48,56},{56,64},{64,7... | collective-permute-start | bytes 786440 | tf_op jit(solution)/shard_map/ppermute | solution.py:229
  6.6 0.7 %copy-start.5 = (bf16[128,64]{0,1:T(8,128)(2,1)S(1)}, bf16[128,64]{0,1:T(8,128)(2,1)}, u32[]{:S(2)}) copy-start(bf16[128,64]{0,1:T(8,128)(2,1)} %param.16) | copy-start | bytes 49156
  10.4 31.4 %copy-start.2 = (bf16[128,1024]{1,0:T(8,128)(2,1)S(1)}, bf16[128,1024]{1,0:T(8,128)(2,1)}, u32[]{:S(2)}) copy-start(bf16[128,1024]{1,0:T(8,128)(2,1)} %hidden_ref.1) | copy-start | bytes 786436
  10.4 31.4 %copy-start.3 = (bf16[128,1024]{1,0:T(8,128)(2,1)S(1)}, bf16[128,1024]{1,0:T(8,128)(2,1)}, u32[]{:S(2)}) copy-start(bf16[128,1024]{1,0:T(8,128)(2,1)} %query_ref.3) | copy-start | bytes 786436
  10.4 31.4 %copy-start.4 = (f32[1024]{0:T(1024)S(1)}, f32[1024]{0:T(1024)}, u32[]{:S(2)}) copy-start(f32[1024]{0:T(1024)} %param.19) | copy-start | bytes 12292

commit v2 on v1

v2 whole, which is shorter than its diff:
```python
import jax
import jax.numpy as jnp
from jax import lax
from jax.experimental import pallas as pl
from jax.experimental.pallas import tpu as pltpu
from jax.sharding import Mesh, PartitionSpec as P

F32 = jnp.float32
BF16 = jnp.bfloat16
LANES = 128
SUBS = 8
STEP = 16
JUMPS = (1, 2, 4)
MODES = 8
SEQ = ("y", "x", "core")
VMEM_LIMIT = 20 * 1024 * 1024


def iota(shape, dim):
    return lax.broadcasted_iota(jnp.int32, shape, dim)


def strided(row):
    return pl.ds(row, SUBS, stride=STEP)


def tile_cols(tile):
    return pl.ds(tile * LANES, LANES)


def spread_row(values, n):
    return jnp.broadcast_to(values[n : n + 1], (SUBS, LANES))


def group_rows(values, width):
    rows, lanes = values.shape
    member = iota((2 * SUBS, lanes), 1) // width
    parts = []
    for part in range(lanes // width):
        mask = (member == part).astype(F32).astype(BF16)
        parts.append(values * jnp.concatenate([mask] * (rows // (2 * SUBS)), 0))
    return jnp.concatenate(parts, 0)


def lost_share(rate):
    square = rate * rate
    series = 1.0 + square / 110.0
    for factor in (72.0, 42.0, 20.0, 6.0):
        series = 1.0 + square / factor * series
    small = 2.0 * jnp.exp(-rate) * rate * series
    return jnp.where(rate < 0.5, small, 1.0 - jnp.exp(-2.0 * rate))


def locate(tile, refs):
    for ref in refs:
        if tile < ref.shape[-1] // LANES:
            return ref, tile
        tile -= ref.shape[-1] // LANES


def part_kernel(first, product_ref, *refs):
    refs[-1][...] = product_ref[:, first : first + refs[-1].shape[1]]


def own_kernel(
    filter_ref, rate_ref, residue_ref, product_0, product_1,
    bands_ref, conv_ref, taps_ref, fade_ref, weights_ref,
):
    groups, taps = filter_ref.shape
    channels = rate_ref.shape[1]
    width = channels // groups
    per_tile = LANES // width
    row, lane = iota((taps, taps), 0), iota((taps, taps), 1)
    flip = ((row + lane) % taps == 0).astype(BF16)
    flipped = jnp.dot(filter_ref[...], flip, preferred_element_type=F32)
    earlier = lane > row
    block = iota((SUBS, LANES), 0)
    for tile in range(channels // LANES):
        cols = tile_cols(tile)
        bands = []
        for part in range(per_tile):
            group = tile * per_tile + part
            one = jnp.broadcast_to(flipped[group : group + 1], (taps, taps))
            circulant = pltpu.roll(one, 0, 1, stride=1, stride_axis=0)
            bands_ref[tile, :, tile_cols(part)] = jnp.where(earlier, circulant, 0.0).astype(BF16)
            bands.append(jnp.where(earlier, 0.0, circulant).astype(BF16))
        product_ref, place = locate(tile, (product_0, product_1))
        product = product_ref[:, tile_cols(place)]
        conv_ref[:, cols] = jnp.dot(
            jnp.concatenate(bands, 1), group_rows(product, width), preferred_element_type=F32
        )
        rate = rate_ref[:, cols]
        gain = residue_ref[:, cols] * jnp.sqrt(lost_share(rate))
        fade = rate * -float(STEP)
        fade_ref[:, cols] = fade
        decay = jnp.exp(fade / STEP)
        powers = gain
        for lag in range(STEP):
            taps_ref[lag : lag + 1, cols] = jnp.sum(powers, 0, keepdims=True)
            powers = powers * decay
        jumps = [jnp.exp(fade * k) for k in JUMPS]
        start = gain * decay
        for n in range(gain.shape[0]):
            weights_ref[0, n, :, cols] = spread_row(decay, n)
            for k, jump in zip(JUMPS, jumps):
                place = JUMPS.index(k) + 1
                weights_ref[place, n, :, cols] = jnp.where(block >= k, spread_row(jump, n), 0.0)
            begin = spread_row(start, n)
            weights_ref[4, n, :, cols] = jnp.where(block >= 1, begin, 0.0)
            reach = jnp.exp(block.astype(F32) * spread_row(fade, n))
            weights_ref[5, n, :, cols] = begin * reach


def medium_kernel(
    start, halo_ref, bands_ref, conv_ref, query_ref, key_ref, weights_ref, *refs
):
    *others, out_mr_ref, source_ref, starts_ref, state_ref = refs
    poles = weights_ref.shape[1]
    width = LANES * LANES // bands_ref.shape[2]
    states = [other[:, tile_cols(i)] for other in others for i in range(other.shape[1] // LANES)]
    for tile in range(halo_ref.shape[1] // LANES):
        whole = start + tile
        cols, here = tile_cols(whole), tile_cols(tile)
        conv = conv_ref[:, cols] + jnp.dot(
            bands_ref[whole], group_rows(halo_ref[:, here], width), preferred_element_type=F32
        )
        out_mr = (query_ref[:, cols].astype(F32) * conv).astype(BF16)
        out_mr_ref[:, here] = out_mr
        source_ref[tile] = key_ref[:, cols].astype(F32) * out_mr.astype(F32)
        rows = [source_ref[tile, strided(i), :] for i in range(STEP)]
        last = []
        for first in range(0, poles, MODES):
            modes = range(first, min(first + MODES, poles))
            decays = [weights_ref[0, n, :, cols] for n in modes]
            ends = [rows[0]] * len(modes)
            for i in range(1, STEP):
                ends = [end * decay + rows[i] for end, decay in zip(ends, decays)]
            for place, k in enumerate(JUMPS):
                weights = [weights_ref[place + 1, n, :, cols] for n in modes]
                ends = [end + w * pltpu.roll(end, k, 0) for end, w in zip(ends, weights)]
            for n, end in zip(modes, ends):
                starts_ref[n, :, here] = weights_ref[4, n, :, cols] * pltpu.roll(end, 1, 0)
                last.append(end[SUBS - 1 :])
        states.append(jnp.concatenate(last, 0).astype(BF16))
    if not others:
        for tile, state in enumerate(states):
            state_ref[:, tile_cols(tile)] = state
        return
    half = state_ref.shape[2] // LANES
    for tile, state in enumerate(states):
        for to in range(tile // half, state_ref.shape[0], 2):
            state_ref[to, :, tile_cols(tile % half)] = state


def own_half(tile, half):
    start = lax.axis_index("core") * half + tile * LANES
    return pl.ds(pl.multiple_of(start, LANES), LANES)


def tree_sum(values):
    while len(values) > 1:
        values = [a + b for a, b in zip(values[::2], values[1::2])] + values[len(values) // 2 * 2 :]
    return values[0]


def scan_stack(stack_ref, cols, step):
    states = [jnp.zeros(step.shape, F32)]
    for j in range(stack_ref.shape[0]):
        states.append(states[-1] * step + stack_ref[j, :, cols].astype(F32))
    return states


def pick(states, position):
    chosen = states[0]
    for j in range(1, len(states)):
        chosen = jnp.where(position == j, states[j], chosen)
    return chosen


def row_kernel(tokens, stack_ref, fade_ref, ahead_ref, spread_ref):
    half = stack_ref.shape[2]
    for tile in range(half // LANES):
        cols = tile_cols(tile)
        step = jnp.exp(fade_ref[:, own_half(tile, half)] * (tokens // STEP))
        states = scan_stack(stack_ref, cols, step)
        for core in range(2):
            ahead_ref[core, :, cols] = pick(states[core:-1:2], lax.axis_index("x"))
        state = states[-1].astype(BF16)
        for to in range(spread_ref.shape[0]):
            spread_ref[to, :, cols] = state


def join_kernel(tokens, stack_ref, ahead_ref, fade_ref, incoming_ref):
    half = stack_ref.shape[2]
    in_row = lax.axis_size("x") * 2
    first = (lax.axis_index("x") * 2).astype(F32)
    for tile in range(half // LANES):
        cols = tile_cols(tile)
        fade = fade_ref[:, own_half(tile, half)] * (tokens // STEP)
        states = scan_stack(stack_ref, cols, jnp.exp(fade * in_row))
        above = pick(states[:-1], lax.axis_index("y"))
        for core in range(2):
            reach = jnp.exp(fade * (first + core))
            incoming_ref[core, :, cols] = ahead_ref[core, :, cols] + reach * above


def long_kernel(
    incoming_ref, taps_ref, weights_ref, hidden_ref, query_ref, norm_ref,
    out_mr_0, source_0, starts_0, out_mr_1, source_1, starts_1,
    scaled_ref, squares_ref, conv_ref,
):
    tokens, channels = hidden_ref.shape
    poles, half = incoming_ref.shape[2:]
    core = lax.axis_index("core")
    squares = jnp.zeros((tokens, LANES), F32)
    for tile in range(channels // LANES):
        cols = tile_cols(tile)
        out_mr_ref, place = locate(tile, (out_mr_0, out_mr_1))
        source_ref, starts_ref = (source_0, starts_0) if out_mr_ref is out_mr_0 else (source_1, starts_1)
        here = tile_cols(place)
        side = tile * LANES // half
        incoming = incoming_ref[side, core, :, tile_cols(tile % (half // LANES))]
        rows = [source_ref[place, strided(i), :] for i in range(STEP)]
        sums = [jnp.zeros((SUBS, LANES), F32)] * STEP
        for lag in range(STEP):
            tap = jnp.broadcast_to(taps_ref[lag : lag + 1, cols], (SUBS, LANES))
            for i in range(lag, STEP):
                sums[i] = sums[i] + tap * rows[i - lag]
        for first in range(0, poles, MODES):
            modes = range(first, min(first + MODES, poles))
            decays = [weights_ref[0, n, :, cols] for n in modes]
            values = [
                starts_ref[n, :, here] + weights_ref[5, n, :, cols] * spread_row(incoming, n)
                for n in modes
            ]
            for i in range(STEP):
                if i:
                    values = [value * decay for value, decay in zip(values, decays)]
                sums[i] = sums[i] + tree_sum(values)
        for i in range(STEP):
            conv_ref[strided(i), :] = sums[i]
        combined = (
            hidden_ref[:, cols].astype(F32)
            + out_mr_ref[:, here].astype(F32)
            + query_ref[:, cols].astype(F32) * conv_ref[...]
        )
        scaled_ref[:, cols] = combined * norm_ref[:, cols]
        squares = squares + combined * combined
    total = jnp.sum(squares.T, 0, keepdims=True)
    squares_ref[...] = jnp.broadcast_to(total, squares_ref.shape)


def norm_kernel(total, scaled_ref, squares_ref, out_ref):
    tokens, channels = scaled_ref.shape
    square = jnp.sum(squares_ref[...], 0, keepdims=True)
    inverse = jnp.broadcast_to(lax.rsqrt(square / total + 1e-06), (tokens, tokens)).T
    for tile in range(channels // LANES):
        cols = tile_cols(tile)
        out_ref[:, cols] = (scaled_ref[:, cols] * inverse).astype(BF16)


def call(kernel, outs, scratch=(), cost=None):
    return pl.pallas_call(
        kernel,
        out_shape=[jax.ShapeDtypeStruct(shape, dtype) for shape, dtype in outs],
        scratch_shapes=[pltpu.VMEM(shape, dtype) for shape, dtype in scratch],
        compiler_params=pltpu.CompilerParams(vmem_limit_bytes=VMEM_LIMIT),
        cost_estimate=cost,
    )


def per_device(
    hidden_in,
    query_mr,
    key_mr,
    value_mr,
    query_li,
    key_li,
    mr_filter,
    li_rate,
    li_residue,
    norm_gain,
):
    tokens, channels = key_mr.shape
    filter_len, groups = mr_filter.shape
    poles = li_rate.shape[0]
    tiles = channels // LANES
    half = channels // 2
    ys = lax.axis_size("y")
    in_row = lax.axis_size("x") * lax.axis_size("core")
    long_op = pl.CostEstimate(
        flops=16 * groups * filter_len * filter_len * LANES, bytes_accessed=2**22, transcendentals=0
    )
    product = (key_mr.astype(F32) * value_mr.astype(F32)).astype(BF16)
    route = [(i, i + 1) for i in range(ys * in_row - 1)]
    cut = tiles * 5 // 8
    sizes = ((0, cut), (cut, tiles - cut))
    parts = []
    for first, size in sizes:
        parts += call(
            lambda *refs, first=first: part_kernel(first * LANES, *refs),
            [((tokens, size * LANES), BF16)],
            cost=long_op,
        )(product, *parts)
    halos = [lax.ppermute(part, SEQ, route) for part in parts]
    bands, own, taps, fade, weights = call(
        own_kernel,
        [
            ((tiles, filter_len, LANES * groups * LANES // channels), BF16),
            ((tokens, channels), F32),
            ((STEP, channels), F32),
            ((poles, channels), F32),
            ((6, poles, SUBS, channels), F32),
        ],
        cost=long_op,
    )(mr_filter.T, li_rate, li_residue, *parts)
    done, states = [], []
    for (first, size), halo in zip(sizes, halos):
        last = first + size == tiles
        *mixed, state = call(
            lambda *refs, first=first: medium_kernel(first, *refs),
            [
                ((tokens, size * LANES), BF16),
                ((size, tokens, LANES), F32),
                ((poles, SUBS, size * LANES), F32),
                ((in_row, poles, half) if last else (poles, size * LANES), BF16),
            ],
        )(halo, bands, own, query_mr, key_li, weights, *states)
        done += mixed
        states = [state]
    (states,) = states
    states = lax.all_to_all(states, ("x", "core"), 0, 0, tiled=True)
    ahead, rows = call(
        lambda *refs: row_kernel(tokens, *refs),
        [((2, poles, half), F32), ((ys, poles, half), BF16)],
    )(states, fade)
    rows = lax.all_to_all(rows, "y", 0, 0, tiled=True)
    (incoming,) = call(lambda *refs: join_kernel(tokens, *refs), [((2, poles, half), F32)])(
        rows, ahead, fade
    )
    incoming = lax.all_gather(incoming, "core")
    scaled, squares = call(
        long_kernel,
        [((tokens, channels), F32), ((SUBS, tokens), F32)],
        [((tokens, LANES), F32)],
    )(
        incoming, taps, weights, hidden_in, query_li, norm_gain.reshape(1, channels), *done
    )
    chans = lax.axis_size("chan")
    squares = lax.all_to_all(squares.reshape(chans, 1, tokens), "chan", 0, 0, tiled=True)
    (out,) = call(
        lambda *refs: norm_kernel(channels * chans, *refs), [((tokens, channels), BF16)]
    )(scaled, squares.reshape(chans, tokens))
    return out


def solution(mesh):
    seq, chan = mesh.devices.shape
    xs = 4 if seq >= 64 else 2
    fine = Mesh(mesh.devices.reshape(seq // (2 * xs), xs, 2, chan), ("y", "x", "core", "chan"))
    both = P(SEQ, "chan")
    last = P(None, "chan")
    return jax.shard_map(
        per_device,
        mesh=fine,
        in_specs=(both,) * 6 + (last,) * 3 + (P("chan"),),
        out_specs=both,
        check_vma=False,
    )
```

time: 60.7 us -> 59.7 us (0.984)
  starting transfers between devices: 4.51 us -> 6.56 us
  other arithmetic: 2.93 us -> 1.09 us
  Pallas kernels: 4.73 us -> 5.8 us
  blocking collectives: 45.8 us -> 44.8 us
  waiting for transfers between devices: 1.66 us -> 0.87 us
  local copies, waits for them, and re-layouts: 0.73 us -> 0.04 us
    ppermute x1 -> x2, starting transfers between devices: 4.51 us -> 6.56 us  [per_device(): halos = [lax.ppermute(part, SEQ, route) for part in parts]]
    pallas_call x2 -> x6, Pallas kernels: 3.18 us -> 4.39 us  [the longest x1 1.79 us: per_device(): call(own_kernel, [((tiles, filter_len, LANES * groups * LANES // channels...]
    all_to_all x1, blocking collectives: 15.7 us -> 14.7 us  [per_device(): rows = lax.all_to_all(rows, 'y', 0, 0, tiled=True)]
    another operation x2 -> x0, other arithmetic: 0.94 us -> none  [per_device(): table = jnp.stack([gain, li_rate * -float(STEP)])]
    convert_element_type x1 -> x0, other arithmetic: 0.81 us -> none  [per_device(): return (scaled * inverse_rms[:, None]).astype(BF16)]
    ppermute x1 -> x2, waiting for transfers between devices: 1.66 us -> 0.87 us  [per_device(): halos = [lax.ppermute(part, SEQ, route) for part in parts]]
    unnamed x12 -> x16, local copies, waits for them, and re-layouts: 0.73 us -> 0.04 us
  transfers between devices with their start and end apart: 1 -> 2, of which waited for: 1 -> 2; matrix products, arithmetic and copies ran while one was open for 2% -> 0% of each run, Pallas kernels for 2% -> 5%
where the time goes in v2:
time: 59.7 us; the launch traced here: 59.4 us
  blocking collectives  44.8 us (75%)
  starting transfers between devices  6.56 us (11%)
  Pallas kernels  5.8 us (10%)
  other arithmetic  1.09 us (2%)
  waiting for transfers between devices  0.87 us (1%)
    all_to_all x1, blocking collectives, per_device(): lax.all_to_all(squares.reshape(chans, 1, tokens), 'chan', 0, 0, tiled=True)  16.4 us
    all_to_all x1, blocking collectives, per_device(): rows = lax.all_to_all(rows, 'y', 0, 0, tiled=True)  14.7 us
    all_to_all x1, blocking collectives, per_device(): states = lax.all_to_all(states, ('x', 'core'), 0, 0, tiled=True)  9.89 us
    ppermute x2, starting transfers between devices, per_device(): halos = [lax.ppermute(part, SEQ, route) for part in parts]  6.56 us
    all_gather x1, blocking collectives, per_device(): incoming = lax.all_gather(incoming, 'core')  3.92 us
    pallas_call x1, Pallas kernels, per_device(): call(own_kernel, [((tiles, filter_len, LANES * groups * LANES // channels...  1.79 us
    pallas_call x2, Pallas kernels, per_device(): call(lambda *refs, first=first: medium_kernel(first, *refs), [((tokens, s...  1.74 us
    pallas_call x1, Pallas kernels, per_device(): call(long_kernel, [((tokens, channels), F32), ((SUBS, tokens), F32)], [((...  1.3 us
  transfers between devices with their start and end apart: 2, of which 2 were waited for; matrix products, arithmetic and copies ran while one was open for 0% of the time, Pallas kernels for 5%

profile of v2, /device:TPU:1, one launch (start us, length us, event | category | flops | bytes accessed | tf_op | source)
XLA Modules:
  0.0 59.4 jit_solution(4119113645007482324)
XLA Ops:
  0.0 1.1 %multiply_convert_fusion.refs_0_ = bf16[128,1024]{1,0:T(8,128)(2,1)S(1)} fusion(bf16[128,1024]{1,0:T(8,128)(2,1)} %param.13, bf16[128,1024]{1,0:T(8,128)(2,1)} %param.12), kind=kLoop, calls=%fused_computation | loop fusion | flops 524288 | bytes 786432 | tf_op jit(solution)/shard_map/convert_element_type | solution.py:294
  1.1 0.0 copy-start.5
  1.1 0.0 copy-start.6
  1.1 0.0 copy-start.7
  1.2 4.6 %collective-permute-start.1 = (bf16[128,640]{1,0:T(8,128)(2,1)S(1)}, bf16[128,640]{1,0:T(8,128)(2,1)S(1)}, u32[]{:S(2)}, u32[]{:S(2)}) collective-permute-start(bf16[128,640]{1,0:T(8,128)(2,1)S(1)} %shard_map.100.refs_1_.product_0), channel_id=1, source_target_pairs={{0,8},{8,16},{16,24},{24,32},{32,40},{40,48},{48,56},{56,64},{64,7... | collective-permute-start | bytes 491528 | tf_op jit(solution)/shard_map/ppermute | solution.py:305
  5.8 1.9 %collective-permute-start = (bf16[128,384]{1,0:T(8,128)(2,1)S(1)}, bf16[128,384]{1,0:T(8,128)(2,1)S(1)}, u32[]{:S(2)}, u32[]{:S(2)}) collective-permute-start(bf16[128,384]{1,0:T(8,128)(2,1)S(1)} %shard_map.101.product_1), channel_id=1, source_target_pairs={{0,8},{8,16},{16,24},{24,32},{32,40},{40,48},{48,56},{56,64},{64,7... | collective-permute-start | bytes 294920 | tf_op jit(solution)/shard_map/ppermute | solution.py:305
  7.8 0.0 copy-done.5
  7.8 0.0 copy-done.6
  7.8 0.0 copy-done.7
  7.8 0.0 copy-start
  7.8 0.0 copy-start.1
  7.8 1.8 %shard_map.102 = (bf16[8,128,1024]{2,1,0:T(8,128)(2,1)S(1)}, f32[128,1024]{1,0:T(8,128)S(1)}, f32[16,1024]{1,0:T(8,128)S(1)}, f32[16,1024]{1,0:T(8,128)S(1)}, f32[6,16,8,1024]{3,2,1,0:T(8,128)S(1)}) custom-call(bf16[64,128]{1,0:T(8,128)(2,1)S(1)} %bitcast.11, f32[16,1024]{1,0:T(8,128)S(1)} %copy-done.5, f32[16,1024]{1,0:T(8,128)S(1)} %copy-done.6, ...), custom_call_target="tpu_custom_call" | custom-call | flops 2147483648 | bytes 4194304 | tf_op jit(solution)/shard_map/pallas_call | solution.py:306
  9.6 0.7 %collective-permute-done.1.refs_0_ = bf16[128,640]{1,0:T(8,128)(2,1)S(1)} collective-permute-done((bf16[128,640]{1,0:T(8,128)(2,1)S(1)}, bf16[128,640]{1,0:T(8,128)(2,1)S(1)}, u32[]{:S(2)}, u32[]{:S(2)}) %collective-permute-start.1) | collective-permute-done | bytes 163872 | tf_op jit(solution)/shard_map/ppermute | solution.py:305
  10.3 0.0 copy-done
  10.3 0.0 copy-done.1
  10.3 1.1 %shard_map.103 = (bf16[128,640]{1,0:T(8,128)(2,1)S(1)}, f32[5,128,128]{2,1,0:T(8,128)S(1)}, f32[16,8,640]{2,1,0:T(8,128)S(1)}, bf16[16,640]{1,0:T(8,128)(2,1)S(1)}) custom-call(bf16[128,640]{1,0:T(8,128)(2,1)S(1)} %collective-permute-done.1.refs_0_, bf16[8,128,1024]{2,1,0:T(8,128)(2,1)S(1)} %get-tuple-element.22.refs_1_, ...), custom_call_target="tpu_custom_call" | custom-call | tf_op jit(solution)/shard_map/pallas_call | solution.py:320
  11.4 0.1 collective-permute-done.refs_0_
  11.6 0.0 copy-start.2
  11.6 0.0 copy-start.3
  11.6 0.0 copy-start.4
  11.6 0.7 %shard_map.104 = (bf16[128,384]{1,0:T(8,128)(2,1)S(1)}, f32[3,128,128]{2,1,0:T(8,128)S(1)}, f32[16,8,384]{2,1,0:T(8,128)S(1)}, bf16[8,16,512]{2,1,0:T(8,128)(2,1)S(1)}) custom-call(bf16[128,384]{1,0:T(8,128)(2,1)S(1)} %collective-permute-done.refs_0_, bf16[8,128,1024]{2,1,0:T(8,128)(2,1)S(1)} %get-tuple-element.22.refs_1_, ...), custom_call_target="tpu_custom_call" | custom-call | tf_op jit(solution)/shard_map/pallas_call | solution.py:320
  12.2 9.9 %all_to_all.15.refs_0_ = bf16[8,16,512]{2,1,0:T(8,128)(2,1)S(1)} all-to-all(bf16[8,16,512]{2,1,0:T(8,128)(2,1)S(1)} %get-tuple-element.26), channel_id=1, replica_groups=mesh['y'=8,'x'=4,'core'=2,'chan'=8] {'x','core'}, dimensions={0} | all-to-all | bytes 262144 | tf_op jit(solution)/shard_map/all_to_all | solution.py:332
  22.1 0.1 shard_map.105
  22.2 14.7 %all_to_all.16.refs_0_ = bf16[8,16,512]{2,1,0:T(8,128)(2,1)S(1)} all-to-all(bf16[8,16,512]{2,1,0:T(8,128)(2,1)S(1)} %get-tuple-element.28), channel_id=1, replica_groups=mesh['y'=8,'x'=4,'core'=2,'chan'=8] {'y'}, dimensions={0} | all-to-all | bytes 262144 | tf_op jit(solution)/shard_map/all_to_all | solution.py:337
  36.9 0.1 shard_map.106
  36.9 3.9 %all-gather = f32[4,16,512]{2,1,0:T(8,128)S(1)} all-gather(f32[2,16,512]{2,1,0:T(8,128)S(1)} %shard_map.106), channel_id=2, replica_groups=mesh['y'=8,'x'=4,'core'=2,'chan'=8] {'core'}, dimensions={0}, use_global_device_ids=true | all-gather | bytes 196608 | tf_op jit(solution)/shard_map/all_gather | solution.py:341
  40.9 0.0 copy-done.2
  40.9 0.0 copy-done.3
  40.9 0.0 copy-done.4
  40.9 1.3 %shard_map.107 = (f32[128,1024]{1,0:T(8,128)S(1)}, f32[8,128]{1,0:T(8,128)S(1)}) custom-call(f32[2,2,16,512]{3,2,1,0:T(8,128)S(1)} %bitcast.7, f32[16,1024]{1,0:T(8,128)S(1)} %get-tuple-element.30.taps_ref, f32[6,16,8,1024]{3,2,1,0:T(8,128)S(1)} %get-tuple-element.24.refs_5_.weights_ref, bf16[128,1024]{1,0:T(8,128)(2,1)S(1)} %copy-done.2, ...), custom_call_target="tpu_custom_call" | custom-call | tf_op jit(solution)/shard_map/pallas_call | solution.py:342
  42.2 16.4 %all_to_all.17 = f32[8,1,128]{2,1,0:T(1,128)S(1)} all-to-all(f32[8,1,128]{2,1,0:T(1,128)S(1)} %bitcast.9), channel_id=1, replica_groups=mesh['y'=8,'x'=4,'core'=2,'chan'=8] {'chan'}, dimensions={0} | all-to-all | bytes 8192 | tf_op jit(solution)/shard_map/all_to_all | solution.py:350
  58.5 0.8 %shard_map.108 = bf16[128,1024]{1,0:T(8,128)(2,1)} custom-call(f32[128,1024]{1,0:T(8,128)S(1)} %get-tuple-element.37.refs_0_, f32[8,128]{1,0:T(8,128)S(1)} %bitcast.8), custom_call_target="tpu_custom_call" | custom-call | tf_op jit(solution)/shard_map/pallas_call | solution.py:351
  (2 shorter events, 0.0 us)
Async XLA Ops:
  1.1 6.6 %copy-start.5 = (f32[16,1024]{1,0:T(8,128)S(1)}, f32[16,1024]{1,0:T(8,128)}, u32[]{:S(2)}) copy-start(f32[16,1024]{1,0:T(8,128)} %rate_ref.1) | copy-start | bytes 196612
  1.1 6.6 %copy-start.6 = (f32[16,1024]{1,0:T(8,128)S(1)}, f32[16,1024]{1,0:T(8,128)}, u32[]{:S(2)}) copy-start(f32[16,1024]{1,0:T(8,128)} %residue_ref.1) | copy-start | bytes 196612
  1.1 6.6 %copy-start.7 = (bf16[128,64]{0,1:T(8,128)(2,1)S(1)}, bf16[128,64]{0,1:T(8,128)(2,1)}, u32[]{:S(2)}) copy-start(bf16[128,64]{0,1:T(8,128)(2,1)} %param.16) | copy-start | bytes 49156
  1.2 9.2 %collective-permute-start.1 = (bf16[128,640]{1,0:T(8,128)(2,1)S(1)}, bf16[128,640]{1,0:T(8,128)(2,1)S(1)}, u32[]{:S(2)}, u32[]{:S(2)}) collective-permute-start(bf16[128,640]{1,0:T(8,128)(2,1)S(1)} %shard_map.100.refs_1_.product_0), channel_id=1, source_target_pairs={{0,8},{8,16},{16,24},{24,32},{32,40},{40,48},{48,56},{56,64},{64,7... | collective-permute-start | bytes 491528 | tf_op jit(solution)/shard_map/ppermute | solution.py:305
  5.8 5.7 %collective-permute-start = (bf16[128,384]{1,0:T(8,128)(2,1)S(1)}, bf16[128,384]{1,0:T(8,128)(2,1)S(1)}, u32[]{:S(2)}, u32[]{:S(2)}) collective-permute-start(bf16[128,384]{1,0:T(8,128)(2,1)S(1)} %shard_map.101.product_1), channel_id=1, source_target_pairs={{0,8},{8,16},{16,24},{24,32},{32,40},{40,48},{48,56},{56,64},{64,7... | collective-permute-start | bytes 294920 | tf_op jit(solution)/shard_map/ppermute | solution.py:305
  7.8 2.6 %copy-start = (bf16[128,1024]{1,0:T(8,128)(2,1)S(1)}, bf16[128,1024]{1,0:T(8,128)(2,1)}, u32[]{:S(2)}) copy-start(bf16[128,1024]{1,0:T(8,128)(2,1)} %refs_3_.3) | copy-start | bytes 786436
  7.8 2.5 %copy-start.1 = (bf16[128,1024]{1,0:T(8,128)(2,1)S(1)}, bf16[128,1024]{1,0:T(8,128)(2,1)}, u32[]{:S(2)}) copy-start(bf16[128,1024]{1,0:T(8,128)(2,1)} %refs_4_.3) | copy-start | bytes 786436
  11.6 29.3 %copy-start.2 = (bf16[128,1024]{1,0:T(8,128)(2,1)S(1)}, bf16[128,1024]{1,0:T(8,128)(2,1)}, u32[]{:S(2)}) copy-start(bf16[128,1024]{1,0:T(8,128)(2,1)} %hidden_ref.1) | copy-start | bytes 786436
  11.6 29.3 %copy-start.3 = (bf16[128,1024]{1,0:T(8,128)(2,1)S(1)}, bf16[128,1024]{1,0:T(8,128)(2,1)}, u32[]{:S(2)}) copy-start(bf16[128,1024]{1,0:T(8,128)(2,1)} %query_ref.1) | copy-start | bytes 786436
  11.6 29.3 %copy-start.4 = (f32[1024]{0:T(1024)S(1)}, f32[1024]{0:T(1024)}, u32[]{:S(2)}) copy-start(f32[1024]{0:T(1024)} %param.19) | copy-start | bytes 12292

commit v3 on v2

--- a/solution.py
+++ b/solution.py
@@ -64,7 +64,7 @@
 
 def own_kernel(
     filter_ref, rate_ref, residue_ref, product_0, product_1,
-    bands_ref, conv_ref, taps_ref, fade_ref, weights_ref,
+    bands_ref, lower_ref, conv_ref, taps_ref, fade_ref, weights_ref,
 ):
     groups, taps = filter_ref.shape
     channels = rate_ref.shape[1]
@@ -74,6 +74,7 @@
     flip = ((row + lane) % taps == 0).astype(BF16)
     flipped = jnp.dot(filter_ref[...], flip, preferred_element_type=F32)
     earlier = lane > row
+    middle = taps // 2
     block = iota((SUBS, LANES), 0)
     for tile in range(channels // LANES):
         cols = tile_cols(tile)
@@ -82,7 +83,14 @@
             group = tile * per_tile + part
             one = jnp.broadcast_to(flipped[group : group + 1], (taps, taps))
             circulant = pltpu.roll(one, 0, 1, stride=1, stride_axis=0)
-            bands_ref[tile, :, tile_cols(part)] = jnp.where(earlier, circulant, 0.0).astype(BF16)
+            band = jnp.where(earlier, circulant, 0.0)
+            bands_ref[tile, :, tile_cols(part)] = band[:middle].astype(BF16)
+            if part % 2 == 0:
+                turned = pltpu.roll(one, middle, 1, stride=1, stride_axis=0)[middle:]
+                left = jnp.where(lane[:middle] > row[:middle], turned, 0.0)
+            else:
+                pair = jnp.where(lane[:middle] < middle, left, band[middle:])
+                lower_ref[tile, :, tile_cols(part // 2)] = pair.astype(BF16)
             bands.append(jnp.where(earlier, 0.0, circulant).astype(BF16))
         product_ref, place = locate(tile, (product_0, product_1))
         product = product_ref[:, tile_cols(place)]
@@ -112,7 +120,7 @@
 
 
 def medium_kernel(
-    start, halo_ref, bands_ref, conv_ref, query_ref, key_ref, weights_ref, *refs
+    start, halo_ref, bands_ref, lower_ref, conv_ref, query_ref, key_ref, weights_ref, *refs
 ):
     *others, out_mr_ref, source_ref, starts_ref, state_ref = refs
     poles = weights_ref.shape[1]
@@ -121,9 +129,12 @@
     for tile in range(halo_ref.shape[1] // LANES):
         whole = start + tile
         cols, here = tile_cols(whole), tile_cols(tile)
-        conv = conv_ref[:, cols] + jnp.dot(
+        upper = jnp.dot(
             bands_ref[whole], group_rows(halo_ref[:, here], width), preferred_element_type=F32
         )
+        later = halo_ref[bands_ref.shape[1] :, here]
+        lower = jnp.dot(lower_ref[whole], group_rows(later, width), preferred_element_type=F32)
+        conv = conv_ref[:, cols] + jnp.concatenate([upper, lower], 0)
         out_mr = (query_ref[:, cols].astype(F32) * conv).astype(BF16)
         out_mr_ref[:, here] = out_mr
         source_ref[tile] = key_ref[:, cols].astype(F32) * out_mr.astype(F32)
@@ -303,10 +314,11 @@
             cost=long_op,
         )(product, *parts)
     halos = [lax.ppermute(part, SEQ, route) for part in parts]
-    bands, own, taps, fade, weights = call(
+    bands, lower, own, taps, fade, weights = call(
         own_kernel,
         [
-            ((tiles, filter_len, LANES * groups * LANES // channels), BF16),
+            ((tiles, filter_len // 2, filter_len * groups // tiles), BF16),
+            ((tiles, filter_len // 2, filter_len // 2 * groups // tiles), BF16),
             ((tokens, channels), F32),
             ((STEP, channels), F32),
             ((poles, channels), F32),
@@ -325,7 +337,7 @@
                 ((poles, SUBS, size * LANES), F32),
                 ((in_row, poles, half) if last else (poles, size * LANES), BF16),
             ],
-        )(halo, bands, own, query_mr, key_li, weights, *states)
+        )(halo, bands, lower, own, query_mr, key_li, weights, *states)
         done += mixed
         states = [state]
     (states,) = states

time: 59.7 us -> 59.6 us (level)
  no operation moved by 1% of the time
where the time goes in v3:
time: 59.6 us; the launch traced here: 59.3 us
  blocking collectives  44.8 us (75%)
  starting transfers between devices  6.56 us (11%)
  Pallas kernels  5.68 us (10%)
  other arithmetic  1.09 us (2%)
  waiting for transfers between devices  0.96 us (2%)
    all_to_all x1, blocking collectives, per_device(): lax.all_to_all(squares.reshape(chans, 1, tokens), 'chan', 0, 0, tiled=True)  16.4 us
    all_to_all x1, blocking collectives, per_device(): rows = lax.all_to_all(rows, 'y', 0, 0, tiled=True)  14.7 us
    all_to_all x1, blocking collectives, per_device(): states = lax.all_to_all(states, ('x', 'core'), 0, 0, tiled=True)  9.81 us
    ppermute x2, starting transfers between devices, per_device(): halos = [lax.ppermute(part, SEQ, route) for part in parts]  6.56 us
    all_gather x1, blocking collectives, per_device(): incoming = lax.all_gather(incoming, 'core')  3.92 us
    pallas_call x1, Pallas kernels, per_device(): call(own_kernel, [((tiles, filter_len // 2, filter_len * groups // tiles)...  1.8 us
    pallas_call x2, Pallas kernels, per_device(): call(lambda *refs, first=first: medium_kernel(first, *refs), [((tokens, s...  1.62 us
    pallas_call x1, Pallas kernels, per_device(): call(long_kernel, [((tokens, channels), F32), ((SUBS, tokens), F32)], [((...  1.29 us
  transfers between devices with their start and end apart: 2, of which 2 were waited for; matrix products, arithmetic and copies ran while one was open for 0% of the time, Pallas kernels for 5%

profile of v3, /device:TPU:1, one launch (start us, length us, event | category | flops | bytes accessed | tf_op | source)
XLA Modules:
  0.0 59.3 jit_solution(463926879304564283)
XLA Ops:
  0.0 1.1 %multiply_convert_fusion.refs_0_ = bf16[128,1024]{1,0:T(8,128)(2,1)S(1)} fusion(bf16[128,1024]{1,0:T(8,128)(2,1)} %param.13, bf16[128,1024]{1,0:T(8,128)(2,1)} %param.12), kind=kLoop, calls=%fused_computation | loop fusion | flops 524288 | bytes 786432 | tf_op jit(solution)/shard_map/convert_element_type | solution.py:305
  1.1 0.0 copy-start.5
  1.1 0.0 copy-start.6
  1.1 0.0 copy-start.7
  1.2 4.6 %collective-permute-start.1 = (bf16[128,640]{1,0:T(8,128)(2,1)S(1)}, bf16[128,640]{1,0:T(8,128)(2,1)S(1)}, u32[]{:S(2)}, u32[]{:S(2)}) collective-permute-start(bf16[128,640]{1,0:T(8,128)(2,1)S(1)} %shard_map.100.refs_1_.product_0), channel_id=1, source_target_pairs={{0,8},{8,16},{16,24},{24,32},{32,40},{40,48},{48,56},{56,64},{64,7... | collective-permute-start | bytes 491528 | tf_op jit(solution)/shard_map/ppermute | solution.py:316
  5.8 1.9 %collective-permute-start = (bf16[128,384]{1,0:T(8,128)(2,1)S(1)}, bf16[128,384]{1,0:T(8,128)(2,1)S(1)}, u32[]{:S(2)}, u32[]{:S(2)}) collective-permute-start(bf16[128,384]{1,0:T(8,128)(2,1)S(1)} %shard_map.101.product_1), channel_id=1, source_target_pairs={{0,8},{8,16},{16,24},{24,32},{32,40},{40,48},{48,56},{56,64},{64,7... | collective-permute-start | bytes 294920 | tf_op jit(solution)/shard_map/ppermute | solution.py:316
  7.8 0.0 copy-done.5
  7.8 0.0 copy-done.6
  7.8 0.0 copy-done.7
  7.8 0.0 copy-start
  7.8 0.0 copy-start.1
  7.8 1.8 %shard_map.102 = (bf16[8,64,1024]{2,1,0:T(8,128)(2,1)S(1)}, bf16[8,64,512]{2,1,0:T(8,128)(2,1)S(1)}, f32[128,1024]{1,0:T(8,128)S(1)}, f32[16,1024]{1,0:T(8,128)S...) custom-call(bf16[64,128]{1,0:T(8,128)(2,1)S(1)} %bitcast.11, f32[16,1024]{1,0:T(8,128)S(1)} %copy-done.5, ...), custom_call_target="tpu_custom_call" | custom-call | flops 2147483648 | bytes 4194304 | tf_op jit(solution)/shard_map/pallas_call | solution.py:317
  9.6 0.7 %collective-permute-done.1.refs_0_ = bf16[128,640]{1,0:T(8,128)(2,1)S(1)} collective-permute-done((bf16[128,640]{1,0:T(8,128)(2,1)S(1)}, bf16[128,640]{1,0:T(8,128)(2,1)S(1)}, u32[]{:S(2)}, u32[]{:S(2)}) %collective-permute-start.1) | collective-permute-done | bytes 163872 | tf_op jit(solution)/shard_map/ppermute | solution.py:316
  10.3 0.0 copy-done
  10.3 0.0 copy-done.1
  10.3 1.0 %shard_map.103 = (bf16[128,640]{1,0:T(8,128)(2,1)S(1)}, f32[5,128,128]{2,1,0:T(8,128)S(1)}, f32[16,8,640]{2,1,0:T(8,128)S(1)}, bf16[16,640]{1,0:T(8,128)(2,1)S(1)}) custom-call(bf16[128,640]{1,0:T(8,128)(2,1)S(1)} %collective-permute-done.1.refs_0_, bf16[8,64,1024]{2,1,0:T(8,128)(2,1)S(1)} %get-tuple-element.23.refs_1_, ...), custom_call_target="tpu_custom_call" | custom-call | tf_op jit(solution)/shard_map/pallas_call | solution.py:332
  11.3 0.2 collective-permute-done.refs_0_
  11.6 0.0 copy-start.2
  11.6 0.0 copy-start.3
  11.6 0.0 copy-start.4
  11.6 0.6 %shard_map.104 = (bf16[128,384]{1,0:T(8,128)(2,1)S(1)}, f32[3,128,128]{2,1,0:T(8,128)S(1)}, f32[16,8,384]{2,1,0:T(8,128)S(1)}, bf16[8,16,512]{2,1,0:T(8,128)(2,1)S(1)}) custom-call(bf16[128,384]{1,0:T(8,128)(2,1)S(1)} %collective-permute-done.refs_0_, bf16[8,64,1024]{2,1,0:T(8,128)(2,1)S(1)} %get-tuple-element.23.refs_1_, ...), custom_call_target="tpu_custom_call" | custom-call | tf_op jit(solution)/shard_map/pallas_call | solution.py:332
  12.2 9.8 %all_to_all.15.refs_0_ = bf16[8,16,512]{2,1,0:T(8,128)(2,1)S(1)} all-to-all(bf16[8,16,512]{2,1,0:T(8,128)(2,1)S(1)} %get-tuple-element.28), channel_id=1, replica_groups=mesh['y'=8,'x'=4,'core'=2,'chan'=8] {'x','core'}, dimensions={0} | all-to-all | bytes 262144 | tf_op jit(solution)/shard_map/all_to_all | solution.py:344
  22.0 0.1 shard_map.105
  22.1 14.7 %all_to_all.16.refs_0_ = bf16[8,16,512]{2,1,0:T(8,128)(2,1)S(1)} all-to-all(bf16[8,16,512]{2,1,0:T(8,128)(2,1)S(1)} %get-tuple-element.30), channel_id=1, replica_groups=mesh['y'=8,'x'=4,'core'=2,'chan'=8] {'y'}, dimensions={0} | all-to-all | bytes 262144 | tf_op jit(solution)/shard_map/all_to_all | solution.py:349
  36.8 0.1 shard_map.106
  36.9 3.9 %all-gather = f32[4,16,512]{2,1,0:T(8,128)S(1)} all-gather(f32[2,16,512]{2,1,0:T(8,128)S(1)} %shard_map.106), channel_id=2, replica_groups=mesh['y'=8,'x'=4,'core'=2,'chan'=8] {'core'}, dimensions={0}, use_global_device_ids=true | all-gather | bytes 196608 | tf_op jit(solution)/shard_map/all_gather | solution.py:353
  40.8 0.0 copy-done.2
  40.8 0.0 copy-done.3
  40.8 0.0 copy-done.4
  40.8 1.3 %shard_map.107 = (f32[128,1024]{1,0:T(8,128)S(1)}, f32[8,128]{1,0:T(8,128)S(1)}) custom-call(f32[2,2,16,512]{3,2,1,0:T(8,128)S(1)} %bitcast.7, f32[16,1024]{1,0:T(8,128)S(1)} %get-tuple-element.32.taps_ref, f32[6,16,8,1024]{3,2,1,0:T(8,128)S(1)} %get-tuple-element.26.refs_6_.weights_ref, bf16[128,1024]{1,0:T(8,128)(2,1)S(1)} %copy-done.2, ...), custom_call_target="tpu_custom_call" | custom-call | tf_op jit(solution)/shard_map/pallas_call | solution.py:354
  42.1 16.4 %all_to_all.17 = f32[8,1,128]{2,1,0:T(1,128)S(1)} all-to-all(f32[8,1,128]{2,1,0:T(1,128)S(1)} %bitcast.9), channel_id=1, replica_groups=mesh['y'=8,'x'=4,'core'=2,'chan'=8] {'chan'}, dimensions={0} | all-to-all | bytes 8192 | tf_op jit(solution)/shard_map/all_to_all | solution.py:362
  58.5 0.8 %shard_map.108 = bf16[128,1024]{1,0:T(8,128)(2,1)} custom-call(f32[128,1024]{1,0:T(8,128)S(1)} %get-tuple-element.39.refs_0_, f32[8,128]{1,0:T(8,128)S(1)} %bitcast.8), custom_call_target="tpu_custom_call" | custom-call | tf_op jit(solution)/shard_map/pallas_call | solution.py:363
  (2 shorter events, 0.0 us)
Async XLA Ops:
  1.1 6.6 %copy-start.5 = (f32[16,1024]{1,0:T(8,128)S(1)}, f32[16,1024]{1,0:T(8,128)}, u32[]{:S(2)}) copy-start(f32[16,1024]{1,0:T(8,128)} %rate_ref.1) | copy-start | bytes 196612
  1.1 6.6 %copy-start.6 = (f32[16,1024]{1,0:T(8,128)S(1)}, f32[16,1024]{1,0:T(8,128)}, u32[]{:S(2)}) copy-start(f32[16,1024]{1,0:T(8,128)} %residue_ref.1) | copy-start | bytes 196612
  1.1 6.6 %copy-start.7 = (bf16[128,64]{0,1:T(8,128)(2,1)S(1)}, bf16[128,64]{0,1:T(8,128)(2,1)}, u32[]{:S(2)}) copy-start(bf16[128,64]{0,1:T(8,128)(2,1)} %param.16) | copy-start | bytes 49156
  1.2 9.2 %collective-permute-start.1 = (bf16[128,640]{1,0:T(8,128)(2,1)S(1)}, bf16[128,640]{1,0:T(8,128)(2,1)S(1)}, u32[]{:S(2)}, u32[]{:S(2)}) collective-permute-start(bf16[128,640]{1,0:T(8,128)(2,1)S(1)} %shard_map.100.refs_1_.product_0), channel_id=1, source_target_pairs={{0,8},{8,16},{16,24},{24,32},{32,40},{40,48},{48,56},{56,64},{64,7... | collective-permute-start | bytes 491528 | tf_op jit(solution)/shard_map/ppermute | solution.py:316
  5.8 5.7 %collective-permute-start = (bf16[128,384]{1,0:T(8,128)(2,1)S(1)}, bf16[128,384]{1,0:T(8,128)(2,1)S(1)}, u32[]{:S(2)}, u32[]{:S(2)}) collective-permute-start(bf16[128,384]{1,0:T(8,128)(2,1)S(1)} %shard_map.101.product_1), channel_id=1, source_target_pairs={{0,8},{8,16},{16,24},{24,32},{32,40},{40,48},{48,56},{56,64},{64,7... | collective-permute-start | bytes 294920 | tf_op jit(solution)/shard_map/ppermute | solution.py:316
  7.8 2.6 %copy-start = (bf16[128,1024]{1,0:T(8,128)(2,1)S(1)}, bf16[128,1024]{1,0:T(8,128)(2,1)}, u32[]{:S(2)}) copy-start(bf16[128,1024]{1,0:T(8,128)(2,1)} %refs_4_.3) | copy-start | bytes 786436
  7.8 2.5 %copy-start.1 = (bf16[128,1024]{1,0:T(8,128)(2,1)S(1)}, bf16[128,1024]{1,0:T(8,128)(2,1)}, u32[]{:S(2)}) copy-start(bf16[128,1024]{1,0:T(8,128)(2,1)} %refs_5_.3) | copy-start | bytes 786436
  11.6 29.3 %copy-start.2 = (bf16[128,1024]{1,0:T(8,128)(2,1)S(1)}, bf16[128,1024]{1,0:T(8,128)(2,1)}, u32[]{:S(2)}) copy-start(bf16[128,1024]{1,0:T(8,128)(2,1)} %hidden_ref.1) | copy-start | bytes 786436
  11.6 29.3 %copy-start.3 = (bf16[128,1024]{1,0:T(8,128)(2,1)S(1)}, bf16[128,1024]{1,0:T(8,128)(2,1)}, u32[]{:S(2)}) copy-start(bf16[128,1024]{1,0:T(8,128)(2,1)} %query_ref.1) | copy-start | bytes 786436
  11.6 29.3 %copy-start.4 = (f32[1024]{0:T(1024)S(1)}, f32[1024]{0:T(1024)}, u32[]{:S(2)}) copy-start(f32[1024]{0:T(1024)} %param.19) | copy-start | bytes 12292

commit v4 on v3

--- a/solution.py
+++ b/solution.py
@@ -78,7 +78,7 @@
     block = iota((SUBS, LANES), 0)
     for tile in range(channels // LANES):
         cols = tile_cols(tile)
-        bands = []
+        bands, tops = [], []
         for part in range(per_tile):
             group = tile * per_tile + part
             one = jnp.broadcast_to(flipped[group : group + 1], (taps, taps))
@@ -91,10 +91,20 @@
             else:
                 pair = jnp.where(lane[:middle] < middle, left, band[middle:])
                 lower_ref[tile, :, tile_cols(part // 2)] = pair.astype(BF16)
-            bands.append(jnp.where(earlier, 0.0, circulant).astype(BF16))
+            own = jnp.where(earlier, 0.0, circulant)
+            bands.append(own[middle:].astype(BF16))
+            if part % 2 == 0:
+                near = own[:middle]
+            else:
+                turned = pltpu.roll(one, middle, 1, stride=1, stride_axis=0)[:middle]
+                right = jnp.where(lane[:middle] - middle <= row[:middle], turned, 0.0)
+                tops.append(jnp.where(lane[:middle] < middle, near, right).astype(BF16))
         product_ref, place = locate(tile, (product_0, product_1))
         product = product_ref[:, tile_cols(place)]
-        conv_ref[:, cols] = jnp.dot(
+        conv_ref[:middle, cols] = jnp.dot(
+            jnp.concatenate(tops, 1), group_rows(product[:middle], width), preferred_element_type=F32
+        )
+        conv_ref[middle:, cols] = jnp.dot(
             jnp.concatenate(bands, 1), group_rows(product, width), preferred_element_type=F32
         )
         rate = rate_ref[:, cols]

time: 59.6 us -> 59.6 us (level)
  no operation moved by 1% of the time
where the time goes in v4:
time: 59.6 us; the launch traced here: 59.3 us
  blocking collectives  44.8 us (75%)
  starting transfers between devices  6.56 us (11%)
  Pallas kernels  5.81 us (10%)
  other arithmetic  1.09 us (2%)
  waiting for transfers between devices  0.83 us (1%)
    all_to_all x1, blocking collectives, per_device(): lax.all_to_all(squares.reshape(chans, 1, tokens), 'chan', 0, 0, tiled=True)  16.4 us
    all_to_all x1, blocking collectives, per_device(): rows = lax.all_to_all(rows, 'y', 0, 0, tiled=True)  14.6 us
    all_to_all x1, blocking collectives, per_device(): states = lax.all_to_all(states, ('x', 'core'), 0, 0, tiled=True)  9.94 us
    ppermute x2, starting transfers between devices, per_device(): halos = [lax.ppermute(part, SEQ, route) for part in parts]  6.56 us
    all_gather x1, blocking collectives, per_device(): incoming = lax.all_gather(incoming, 'core')  3.92 us
    pallas_call x1, Pallas kernels, per_device(): call(own_kernel, [((tiles, filter_len // 2, filter_len * groups // tiles)...  1.92 us
    pallas_call x2, Pallas kernels, per_device(): call(lambda *refs, first=first: medium_kernel(first, *refs), [((tokens, s...  1.62 us
    pallas_call x1, Pallas kernels, per_device(): call(long_kernel, [((tokens, channels), F32), ((SUBS, tokens), F32)], [((...  1.29 us
  transfers between devices with their start and end apart: 2, of which 2 were waited for; matrix products, arithmetic and copies ran while one was open for 0% of the time, Pallas kernels for 5%

profile of v4, /device:TPU:1, one launch (start us, length us, event | category | flops | bytes accessed | tf_op | source)
XLA Modules:
  0.0 59.3 jit_solution(1338673826555896562)
XLA Ops:
  0.0 1.1 %multiply_convert_fusion.refs_0_ = bf16[128,1024]{1,0:T(8,128)(2,1)S(1)} fusion(bf16[128,1024]{1,0:T(8,128)(2,1)} %param.13, bf16[128,1024]{1,0:T(8,128)(2,1)} %param.12), kind=kLoop, calls=%fused_computation | loop fusion | flops 524288 | bytes 786432 | tf_op jit(solution)/shard_map/convert_element_type | solution.py:315
  1.1 0.0 copy-start.5
  1.1 0.0 copy-start.6
  1.1 0.0 copy-start.7
  1.2 4.6 %collective-permute-start.1 = (bf16[128,640]{1,0:T(8,128)(2,1)S(1)}, bf16[128,640]{1,0:T(8,128)(2,1)S(1)}, u32[]{:S(2)}, u32[]{:S(2)}) collective-permute-start(bf16[128,640]{1,0:T(8,128)(2,1)S(1)} %shard_map.100.refs_1_.product_0), channel_id=1, source_target_pairs={{0,8},{8,16},{16,24},{24,32},{32,40},{40,48},{48,56},{56,64},{64,7... | collective-permute-start | bytes 491528 | tf_op jit(solution)/shard_map/ppermute | solution.py:326
  5.8 1.9 %collective-permute-start = (bf16[128,384]{1,0:T(8,128)(2,1)S(1)}, bf16[128,384]{1,0:T(8,128)(2,1)S(1)}, u32[]{:S(2)}, u32[]{:S(2)}) collective-permute-start(bf16[128,384]{1,0:T(8,128)(2,1)S(1)} %shard_map.101.product_1), channel_id=1, source_target_pairs={{0,8},{8,16},{16,24},{24,32},{32,40},{40,48},{48,56},{56,64},{64,7... | collective-permute-start | bytes 294920 | tf_op jit(solution)/shard_map/ppermute | solution.py:326
  7.8 0.0 copy-done.5
  7.8 0.0 copy-done.6
  7.8 0.0 copy-done.7
  7.8 0.0 copy-start
  7.8 0.0 copy-start.1
  7.8 1.9 %shard_map.102 = (bf16[8,64,1024]{2,1,0:T(8,128)(2,1)S(1)}, bf16[8,64,512]{2,1,0:T(8,128)(2,1)S(1)}, f32[128,1024]{1,0:T(8,128)S(1)}, f32[16,1024]{1,0:T(8,128)S...) custom-call(bf16[64,128]{1,0:T(8,128)(2,1)S(1)} %bitcast.11, f32[16,1024]{1,0:T(8,128)S(1)} %copy-done.5, ...), custom_call_target="tpu_custom_call" | custom-call | flops 2147483648 | bytes 4194304 | tf_op jit(solution)/shard_map/pallas_call | solution.py:327
  9.7 0.6 %collective-permute-done.1.refs_0_ = bf16[128,640]{1,0:T(8,128)(2,1)S(1)} collective-permute-done((bf16[128,640]{1,0:T(8,128)(2,1)S(1)}, bf16[128,640]{1,0:T(8,128)(2,1)S(1)}, u32[]{:S(2)}, u32[]{:S(2)}) %collective-permute-start.1) | collective-permute-done | bytes 163872 | tf_op jit(solution)/shard_map/ppermute | solution.py:326
  10.3 0.0 copy-done
  10.3 0.0 copy-done.1
  10.3 1.0 %shard_map.103 = (bf16[128,640]{1,0:T(8,128)(2,1)S(1)}, f32[5,128,128]{2,1,0:T(8,128)S(1)}, f32[16,8,640]{2,1,0:T(8,128)S(1)}, bf16[16,640]{1,0:T(8,128)(2,1)S(1)}) custom-call(bf16[128,640]{1,0:T(8,128)(2,1)S(1)} %collective-permute-done.1.refs_0_, bf16[8,64,1024]{2,1,0:T(8,128)(2,1)S(1)} %get-tuple-element.23.refs_1_, ...), custom_call_target="tpu_custom_call" | custom-call | tf_op jit(solution)/shard_map/pallas_call | solution.py:342
  11.3 0.2 collective-permute-done.refs_0_
  11.6 0.0 copy-start.2
  11.6 0.0 copy-start.3
  11.6 0.0 copy-start.4
  11.6 0.6 %shard_map.104 = (bf16[128,384]{1,0:T(8,128)(2,1)S(1)}, f32[3,128,128]{2,1,0:T(8,128)S(1)}, f32[16,8,384]{2,1,0:T(8,128)S(1)}, bf16[8,16,512]{2,1,0:T(8,128)(2,1)S(1)}) custom-call(bf16[128,384]{1,0:T(8,128)(2,1)S(1)} %collective-permute-done.refs_0_, bf16[8,64,1024]{2,1,0:T(8,128)(2,1)S(1)} %get-tuple-element.23.refs_1_, ...), custom_call_target="tpu_custom_call" | custom-call | tf_op jit(solution)/shard_map/pallas_call | solution.py:342
  12.2 9.9 %all_to_all.15.refs_0_ = bf16[8,16,512]{2,1,0:T(8,128)(2,1)S(1)} all-to-all(bf16[8,16,512]{2,1,0:T(8,128)(2,1)S(1)} %get-tuple-element.28), channel_id=1, replica_groups=mesh['y'=8,'x'=4,'core'=2,'chan'=8] {'x','core'}, dimensions={0} | all-to-all | bytes 262144 | tf_op jit(solution)/shard_map/all_to_all | solution.py:354
  22.2 0.1 shard_map.105
  22.2 14.6 %all_to_all.16.refs_0_ = bf16[8,16,512]{2,1,0:T(8,128)(2,1)S(1)} all-to-all(bf16[8,16,512]{2,1,0:T(8,128)(2,1)S(1)} %get-tuple-element.30), channel_id=1, replica_groups=mesh['y'=8,'x'=4,'core'=2,'chan'=8] {'y'}, dimensions={0} | all-to-all | bytes 262144 | tf_op jit(solution)/shard_map/all_to_all | solution.py:359
  36.8 0.1 shard_map.106
  36.9 3.9 %all-gather = f32[4,16,512]{2,1,0:T(8,128)S(1)} all-gather(f32[2,16,512]{2,1,0:T(8,128)S(1)} %shard_map.106), channel_id=2, replica_groups=mesh['y'=8,'x'=4,'core'=2,'chan'=8] {'core'}, dimensions={0}, use_global_device_ids=true | all-gather | bytes 196608 | tf_op jit(solution)/shard_map/all_gather | solution.py:363
  40.8 0.0 copy-done.2
  40.8 0.0 copy-done.3
  40.8 0.0 copy-done.4
  40.8 1.3 %shard_map.107 = (f32[128,1024]{1,0:T(8,128)S(1)}, f32[8,128]{1,0:T(8,128)S(1)}) custom-call(f32[2,2,16,512]{3,2,1,0:T(8,128)S(1)} %bitcast.7, f32[16,1024]{1,0:T(8,128)S(1)} %get-tuple-element.32.taps_ref, f32[6,16,8,1024]{3,2,1,0:T(8,128)S(1)} %get-tuple-element.26.refs_6_.weights_ref, bf16[128,1024]{1,0:T(8,128)(2,1)S(1)} %copy-done.2, ...), custom_call_target="tpu_custom_call" | custom-call | tf_op jit(solution)/shard_map/pallas_call | solution.py:364
  42.1 16.4 %all_to_all.17 = f32[8,1,128]{2,1,0:T(1,128)S(1)} all-to-all(f32[8,1,128]{2,1,0:T(1,128)S(1)} %bitcast.9), channel_id=1, replica_groups=mesh['y'=8,'x'=4,'core'=2,'chan'=8] {'chan'}, dimensions={0} | all-to-all | bytes 8192 | tf_op jit(solution)/shard_map/all_to_all | solution.py:372
  58.5 0.8 %shard_map.108 = bf16[128,1024]{1,0:T(8,128)(2,1)} custom-call(f32[128,1024]{1,0:T(8,128)S(1)} %get-tuple-element.39.refs_0_, f32[8,128]{1,0:T(8,128)S(1)} %bitcast.8), custom_call_target="tpu_custom_call" | custom-call | tf_op jit(solution)/shard_map/pallas_call | solution.py:373
  (2 shorter events, 0.0 us)
Async XLA Ops:
  1.1 6.6 %copy-start.5 = (f32[16,1024]{1,0:T(8,128)S(1)}, f32[16,1024]{1,0:T(8,128)}, u32[]{:S(2)}) copy-start(f32[16,1024]{1,0:T(8,128)} %rate_ref.1) | copy-start | bytes 196612
  1.1 6.6 %copy-start.6 = (f32[16,1024]{1,0:T(8,128)S(1)}, f32[16,1024]{1,0:T(8,128)}, u32[]{:S(2)}) copy-start(f32[16,1024]{1,0:T(8,128)} %residue_ref.1) | copy-start | bytes 196612
  1.1 6.6 %copy-start.7 = (bf16[128,64]{0,1:T(8,128)(2,1)S(1)}, bf16[128,64]{0,1:T(8,128)(2,1)}, u32[]{:S(2)}) copy-start(bf16[128,64]{0,1:T(8,128)(2,1)} %param.16) | copy-start | bytes 49156
  1.2 9.2 %collective-permute-start.1 = (bf16[128,640]{1,0:T(8,128)(2,1)S(1)}, bf16[128,640]{1,0:T(8,128)(2,1)S(1)}, u32[]{:S(2)}, u32[]{:S(2)}) collective-permute-start(bf16[128,640]{1,0:T(8,128)(2,1)S(1)} %shard_map.100.refs_1_.product_0), channel_id=1, source_target_pairs={{0,8},{8,16},{16,24},{24,32},{32,40},{40,48},{48,56},{56,64},{64,7... | collective-permute-start | bytes 491528 | tf_op jit(solution)/shard_map/ppermute | solution.py:326
  5.8 5.7 %collective-permute-start = (bf16[128,384]{1,0:T(8,128)(2,1)S(1)}, bf16[128,384]{1,0:T(8,128)(2,1)S(1)}, u32[]{:S(2)}, u32[]{:S(2)}) collective-permute-start(bf16[128,384]{1,0:T(8,128)(2,1)S(1)} %shard_map.101.product_1), channel_id=1, source_target_pairs={{0,8},{8,16},{16,24},{24,32},{32,40},{40,48},{48,56},{56,64},{64,7... | collective-permute-start | bytes 294920 | tf_op jit(solution)/shard_map/ppermute | solution.py:326
  7.8 2.6 %copy-start = (bf16[128,1024]{1,0:T(8,128)(2,1)S(1)}, bf16[128,1024]{1,0:T(8,128)(2,1)}, u32[]{:S(2)}) copy-start(bf16[128,1024]{1,0:T(8,128)(2,1)} %refs_4_.3) | copy-start | bytes 786436
  7.8 2.5 %copy-start.1 = (bf16[128,1024]{1,0:T(8,128)(2,1)S(1)}, bf16[128,1024]{1,0:T(8,128)(2,1)}, u32[]{:S(2)}) copy-start(bf16[128,1024]{1,0:T(8,128)(2,1)} %refs_5_.3) | copy-start | bytes 786436
  11.6 29.3 %copy-start.2 = (bf16[128,1024]{1,0:T(8,128)(2,1)S(1)}, bf16[128,1024]{1,0:T(8,128)(2,1)}, u32[]{:S(2)}) copy-start(bf16[128,1024]{1,0:T(8,128)(2,1)} %hidden_ref.1) | copy-start | bytes 786436
  11.6 29.3 %copy-start.3 = (bf16[128,1024]{1,0:T(8,128)(2,1)S(1)}, bf16[128,1024]{1,0:T(8,128)(2,1)}, u32[]{:S(2)}) copy-start(bf16[128,1024]{1,0:T(8,128)(2,1)} %query_ref.1) | copy-start | bytes 786436
  11.6 29.3 %copy-start.4 = (f32[1024]{0:T(1024)S(1)}, f32[1024]{0:T(1024)}, u32[]{:S(2)}) copy-start(f32[1024]{0:T(1024)} %param.19) | copy-start | bytes 12292
